TPU v7x, 512 devices: a whole 4x4x16 slice. The times are simulated.
512 devices in a mesh: cp: 16 (over y, x_hi, core), ep: 32 (over x_lo, z).
Axes of the slice: x: 4 (x_hi: 2, x_lo: 2; x = x_hi * 2 + x_lo), y: 4, z: 16, core: 2. Of those that a mesh axis runs over, the one named last changes fastest.
Arguments:
- query_act: bfloat16 [2048, 12288], P('cp', 'ep'), may hold values from -6 to 6
- key_act: bfloat16 [2048, 12288], P('cp', 'ep'), may hold values from -6 to 6
- value_act: bfloat16 [2048, 8192], P('cp', 'ep'), may hold values from -6 to 6
- out_grad: bfloat16 [2048, 8192], P('cp', 'ep'), may hold values from -24 to 24
- attn_out: bfloat16 [2048, 8192], P('cp', 'ep'), may hold values from -0.59765625 to 0.59765625
- log_norm: float32 [64, 2048], P('ep', 'cp'), may hold values from 0 to 20
- layer_grad: bfloat16 [2048, 7168], P('cp', 'ep'), may hold values from -6 to 6
- gate_probs: float32 [2048, 8], P('cp'), may hold values from 0.05 to 1
- expert_ids: int32 [2048, 8], P('cp'), may hold values from 0 to 31, all different within a row; in each aligned block of 128 rows (0 to 127, 128 to 255, ...) at most 64 rows name the same one
- hidden_acts: bfloat16 [32, 1024, 2048], P('ep', 'cp'), may hold values from -1.5 to 1.5
Outputs:
- query_grad: bfloat16 [2048, 12288], P('cp', 'ep')
- key_grad: bfloat16 [2048, 12288], P('cp', 'ep')
- value_grad: bfloat16 [2048, 8192], P('cp', 'ep')
- down_grad: bfloat16 [32, 2048, 7168], P('ep', None, 'cp')
Inputs may be any that keep to these rules, and one draw needn't show every extreme that they name: `expert_ids`: in each aligned block of 128 rows (the rows of one index of cp), no expert is named by more than 64 rows, a bound that some block reaches; a row names 8 different experts.
All inputs are finite; a program needn't handle non-finite values.
Results may differ from a plain program's by a relative error of at most 0.0064.
Values may be sent and summed in bfloat16 or wider, within the bound.
A program may use at most 64 MiB of HBM per device.

v0:
```python
import jax
import jax.numpy as jnp
from jax import lax
from jax.sharding import PartitionSpec as P

D = 7168
QK = 192
DH = 128
EXPERTS = 32
CAP = 64


def shifted(block, axis, distance):
    devices = range(lax.axis_size(axis))
    route = [(i - distance, i) for i in devices if i - distance in devices]
    return lax.ppermute(block, axis, route)


def passed_along(block, axis, distance):
    devices = range(lax.axis_size(axis))
    route = [((i - distance) % len(devices), i) for i in devices]
    return lax.ppermute(block, axis, route)


def block_grads(q_rows, do_rows, norm_rows, delta_rows, k_rows, v_rows, q_start, k_start):
    scale = QK ** (-0.5)
    count = q_rows.shape[0]
    scores = scale * jnp.einsum("qhd,khd->hqk", q_rows, k_rows, preferred_element_type=jnp.float32)
    q_pos = q_start + jnp.arange(count, dtype=jnp.int32)
    k_pos = k_start + jnp.arange(count, dtype=jnp.int32)
    causal = q_pos[:, None] >= k_pos[None, :]
    probs = jnp.where(causal[None], jnp.exp(scores - norm_rows[:, :, None]), 0.0)
    dprobs = jnp.einsum("qhd,khd->hqk", do_rows, v_rows, preferred_element_type=jnp.float32)
    dscores = (probs * (dprobs - delta_rows[:, :, None])).astype(jnp.bfloat16)
    probs_low = probs.astype(jnp.bfloat16)
    value_part = jnp.einsum("hqk,qhd->khd", probs_low, do_rows, preferred_element_type=jnp.float32)
    key_part = scale * jnp.einsum(
        "hqk,qhd->khd", dscores, q_rows, preferred_element_type=jnp.float32
    )
    query_part = scale * jnp.einsum(
        "hqk,khd->qhd", dscores, k_rows, preferred_element_type=jnp.float32
    )
    return (query_part, key_part, value_part)


def dispatch_block(grad_rows, probs, ids):
    width = grad_rows.shape[1]
    flat = ids.reshape(-1)
    onehot = (flat[:, None] == jnp.arange(EXPERTS, dtype=jnp.int32)[None, :]).astype(jnp.int32)
    before = jnp.cumsum(onehot, axis=0) - onehot
    slot = jnp.sum(before * onehot, axis=1)
    target = flat * CAP + slot
    slot_rows = (probs[:, :, None] * grad_rows[:, None, :].astype(jnp.float32)).astype(jnp.bfloat16)
    slot_rows = slot_rows.reshape(flat.shape[0], width)
    table = (jnp.arange(EXPERTS * CAP, dtype=jnp.int32)[:, None] == target[None, :]).astype(
        jnp.bfloat16
    )
    return jnp.dot(table, slot_rows, preferred_element_type=jnp.float32).astype(jnp.bfloat16)


def local(
    query_act,
    key_act,
    value_act,
    out_grad,
    attn_out,
    log_norm,
    layer_grad,
    gate_probs,
    expert_ids,
    hidden_acts,
):
    cycle = lax.axis_size("cp")
    own = lax.axis_index("cp")
    count = query_act.shape[0]
    heads = log_norm.shape[0]
    q_own = query_act.reshape(count, heads, QK)
    k_own = key_act.reshape(count, heads, QK)
    v_own = value_act.reshape(count, heads, DH)
    do_own = out_grad.reshape(count, heads, DH)
    out_own = attn_out.reshape(count, heads, DH)
    delta_own = jnp.sum(do_own.astype(jnp.float32) * out_own.astype(jnp.float32), axis=2).T
    zeros_wide = jnp.zeros((count, heads, QK), jnp.float32)
    zeros_value = jnp.zeros((count, heads, DH), jnp.float32)

    def nothing(unused):
        return (zeros_wide, zeros_wide, zeros_value)

    def turn(step, carry):
        k_cur, v_cur, k_acc, v_acc, q_acc = carry
        source = (own - step) % cycle

        def work(unused):
            return block_grads(
                q_own, do_own, log_norm, delta_own, k_cur, v_cur, own * count, source * count
            )

        query_part, key_part, value_part = lax.cond(source <= own, work, nothing, 0)
        k_cur, v_cur = shifted((k_cur, v_cur), "cp", 1)
        k_acc, v_acc = passed_along((k_acc + key_part, v_acc + value_part), "cp", 1)
        return (k_cur, v_cur, k_acc, v_acc, q_acc + query_part)

    finished = lax.fori_loop(0, cycle, turn, (k_own, v_own, zeros_wide, zeros_value, zeros_wide))
    k_total, v_total, q_total = (finished[2], finished[3], finished[4])
    query_grad = q_total.reshape(count, heads * QK).astype(jnp.bfloat16)
    key_grad = k_total.reshape(count, heads * QK).astype(jnp.bfloat16)
    value_grad = v_total.reshape(count, heads * DH).astype(jnp.bfloat16)
    group = lax.axis_size("ep")
    per_device = hidden_acts.shape[0]
    share = layer_grad.shape[1]
    buffer = dispatch_block(layer_grad, gate_probs, expert_ids)
    sent = buffer.reshape(group, per_device, CAP, share)
    columns = lax.all_to_all(
        lax.all_to_all(sent, "ep", split_axis=0, concat_axis=3, tiled=True),
        "cp",
        split_axis=3,
        concat_axis=2,
        tiled=True,
    )
    width_share = D // cycle
    columns = columns.reshape(per_device, cycle * CAP, width_share)
    down_total = jnp.einsum(
        "esf,esd->efd",
        lax.all_gather(hidden_acts, "cp", axis=1, tiled=True),
        columns,
        preferred_element_type=jnp.float32,
    )
    down_grad = down_total.astype(jnp.bfloat16)
    return (query_grad, key_grad, value_grad, down_grad)


def solution(mesh):
    return jax.shard_map(
        local,
        mesh=mesh,
        in_specs=(
            P("cp", "ep"),
            P("cp", "ep"),
            P("cp", "ep"),
            P("cp", "ep"),
            P("cp", "ep"),
            P("ep", "cp"),
            P("cp", "ep"),
            P("cp", None),
            P("cp", None),
            P("ep", "cp", None),
        ),
        out_specs=(P("cp", "ep"), P("cp", "ep"), P("cp", "ep"), P("ep", None, "cp")),
        check_vma=False,
    )
```

profile of v0, /device:TPU:32, one launch (start us, length us, event | category | flops | bytes accessed | tf_op | source)
XLA Modules:
  0.0 495.3 jit_solution(3442896452995903136)
XLA Ops:
  8.9 9.0 %reduce-window.6 = s32[32,8,128]{2,1,0:T(8,128)S(1)} reduce-window(s32[32,8,128]{2,1,0:T(8,128)S(1)} %fusion.27, s32[]{:T(128)} %constant.65.clone.1), window={size=1x1x128 pad=0_0x0_0x127_0}, to_apply=%region_5.6 | reduce-window | flops 4161536 | bytes 262148 | tf_op jit(solution)/shard_map/reduce-window
  23.6 16.3 %all-to-all-start = ((bf16[32,1,64,224]{3,2,1,0:T(8,128)(2,1)}), bf16[32,1,64,224]{3,2,1,0:T(8,128)(2,1)S(1)}, u32[]{:S(2)}, u32[]{:S(2)}) async-start(bf16[32,1,64,224]{3,2,1,0:T(8,128)(2,1)} %bitcast.15), calls=%async_computation | async-start | bytes 2097152 | tf_op jit(solution)/shard_map/all_to_all | solution.py:114
  42.1 52.3 %all-to-all-done = bf16[32,1,64,224]{3,2,1,0:T(8,128)(2,1)S(1)} async-done(((bf16[32,1,64,224]{3,2,1,0:T(8,128)(2,1)}), bf16[32,1,64,224]{3,2,1,0:T(8,128)(2,1)S(1)}, u32[]{:S(2)}, u32[]{:S(2)}) %all-to-all-start) | async-done | bytes 917536 | tf_op jit(solution)/shard_map/all_to_all | solution.py:114
  95.3 5.4 %reshape.125 = bf16[1,1,64,7168]{2,1,0,3:T(2,128)(2,1)} reshape(bf16[1,1,64,32,224]{2,4,3,1,0:T(8,128)(2,1)S(1)} %copy.87) | data formatting | bytes 1835008 | tf_op jit(solution)/shard_map/all_to_all | solution.py:114
  101.3 39.8 %reduce = bf16[7168,64]{1,0:T(8,128)(2,1)S(1)} reduce(bf16[7168,1,1,64]{3,2,1,0:T(2,128)(2,1)} %bitcast.82, bf16[]{:T(256)} %broadcast.72), dimensions={1,2}, to_apply=%bitcast.69.reduce_sub_computation | reduce | bytes 1835010
  143.1 6.8 %all-to-all-start.1 = ((bf16[16,2,14336]{2,1,0:T(2,128)(2,1)}), bf16[16,2,14336]{2,1,0:T(2,128)(2,1)S(1)}, u32[]{:S(2)}, u32[]{:S(2)}) async-start(bf16[16,2,14336]{2,1,0:T(2,128)(2,1)} %reshape.126), calls=%async_computation.1 | async-start | bytes 1835008 | tf_op jit(solution)/shard_map/all_to_all | solution.py:113
  150.0 314.9 %while.24 = (s32[]{:T(128)}, bf16[128,2,192]{0,2,1:T(8,128)(2,1)S(1)}, bf16[128,2,128]{2,0,1:T(8,128)(2,1)S(1)}, f32[128,2,192]{0,2,1:T(8,128)S(1)}, f32[128,2,1...) while((s32[]{:T(128)}, ...), condition=%wide.region_4.5_spmd.clone, body=%wide.region_1.4_spmd.clone.sunk | while | flops 55050512 | bytes 5607990 | solution.py:103
  153.6 5.0 %collective-permute-start.1 = (bf16[128,2,128]{2,0,1:T(8,128)(2,1)}, bf16[128,2,128]{2,0,1:T(8,128)(2,1)S(1)}, u32[]{:S(2)}, u32[]{:S(2)}) collective-permute-start(bf16[128,2,128]{2,0,1:T(8,128)(2,1)} %copy.107), channel_id=1, source_target_pairs={{0,32},{32,64},{64,96},{96,128},{128,160},{160,192},{192,224},{224... | collective-permute-start | bytes 196616 | tf_op jit(solution)/shard_map/while/body/eval_jaxpr/ppermute | solution.py:16
  158.6 3.7 conditional.3
  167.9 6.5 %collective-permute-done.3 = f32[128,2,128]{2,0,1:T(8,128)S(1)} collective-permute-done((f32[128,2,128]{2,0,1:T(8,128)S(1)}, f32[128,2,128]{2,0,1:T(8,128)S(1)}, u32[]{:S(2)}, u32[]{:S(2)}) %collective-permute-start.3) | collective-permute-done | bytes 131104 | tf_op jit(solution)/shard_map/while/body/eval_jaxpr/ppermute | solution.py:22
  179.1 5.6 %collective-permute-start.2 = (f32[128,2,192]{0,2,1:T(8,128)S(1)}, f32[128,2,192]{0,2,1:T(8,128)S(1)}, u32[]{:S(2)}, u32[]{:S(2)}) collective-permute-start(f32[128,2,192]{0,2,1:T(8,128)S(1)} %add.109), channel_id=1, source_target_pairs={{480,0},{0,32},{32,64},{64,96},{96,128},{128,160},{160,192},{192,2... | collective-permute-start | bytes 589832 | tf_op jit(solution)/shard_map/while/body/eval_jaxpr/ppermute | solution.py:22
  184.7 5.9 %collective-permute-start.3 = (f32[128,2,128]{2,0,1:T(8,128)S(1)}, f32[128,2,128]{2,0,1:T(8,128)S(1)}, u32[]{:S(2)}, u32[]{:S(2)}) collective-permute-start(f32[128,2,128]{2,0,1:T(8,128)S(1)} %add.110), channel_id=1, source_target_pairs={{480,0},{0,32},{32,64},{64,96},{96,128},{128,160},{160,192},{192,2... | collective-permute-start | bytes 393224 | tf_op jit(solution)/shard_map/while/body/eval_jaxpr/ppermute | solution.py:22
  190.7 3.9 collective-permute-done.3
  197.2 4.5 collective-permute-start.1
  203.8 7.1 %collective-permute-start.3 = (f32[128,2,128]{2,0,1:T(8,128)S(1)}, f32[128,2,128]{2,0,1:T(8,128)S(1)}, u32[]{:S(2)}, u32[]{:S(2)}) collective-permute-start(f32[128,2,128]{2,0,1:T(8,128)S(1)} %add.110), channel_id=1, source_target_pairs={{480,0},{0,32},{32,64},{64,96},{96,128},{128,160},{160,192},{192,2... | collective-permute-start | bytes 393224 | tf_op jit(solution)/shard_map/while/body/eval_jaxpr/ppermute | solution.py:22
  216.5 5.6 %collective-permute-start.1 = (bf16[128,2,128]{2,0,1:T(8,128)(2,1)}, bf16[128,2,128]{2,0,1:T(8,128)(2,1)S(1)}, u32[]{:S(2)}, u32[]{:S(2)}) collective-permute-start(bf16[128,2,128]{2,0,1:T(8,128)(2,1)} %copy.107), channel_id=1, source_target_pairs={{0,32},{32,64},{64,96},{96,128},{128,160},{160,192},{192,224},{224... | collective-permute-start | bytes 196616 | tf_op jit(solution)/shard_map/while/body/eval_jaxpr/ppermute | solution.py:16
  224.2 5.9 %collective-permute-start.3 = (f32[128,2,128]{2,0,1:T(8,128)S(1)}, f32[128,2,128]{2,0,1:T(8,128)S(1)}, u32[]{:S(2)}, u32[]{:S(2)}) collective-permute-start(f32[128,2,128]{2,0,1:T(8,128)S(1)} %add.110), channel_id=1, source_target_pairs={{480,0},{0,32},{32,64},{64,96},{96,128},{128,160},{160,192},{192,2... | collective-permute-start | bytes 393224 | tf_op jit(solution)/shard_map/while/body/eval_jaxpr/ppermute | solution.py:22
  230.2 4.1 collective-permute-done.3
  238.9 5.8 %collective-permute-start.1 = (bf16[128,2,128]{2,0,1:T(8,128)(2,1)}, bf16[128,2,128]{2,0,1:T(8,128)(2,1)S(1)}, u32[]{:S(2)}, u32[]{:S(2)}) collective-permute-start(bf16[128,2,128]{2,0,1:T(8,128)(2,1)} %copy.107), channel_id=1, source_target_pairs={{0,32},{32,64},{64,96},{96,128},{128,160},{160,192},{192,224},{224... | collective-permute-start | bytes 196616 | tf_op jit(solution)/shard_map/while/body/eval_jaxpr/ppermute | solution.py:16
  250.2 6.6 %collective-permute-done.3 = f32[128,2,128]{2,0,1:T(8,128)S(1)} collective-permute-done((f32[128,2,128]{2,0,1:T(8,128)S(1)}, f32[128,2,128]{2,0,1:T(8,128)S(1)}, u32[]{:S(2)}, u32[]{:S(2)}) %collective-permute-start.3) | collective-permute-done | bytes 131104 | tf_op jit(solution)/shard_map/while/body/eval_jaxpr/ppermute | solution.py:22
  259.4 3.5 collective-permute-start.1
  266.1 6.8 %collective-permute-start.3 = (f32[128,2,128]{2,0,1:T(8,128)S(1)}, f32[128,2,128]{2,0,1:T(8,128)S(1)}, u32[]{:S(2)}, u32[]{:S(2)}) collective-permute-start(f32[128,2,128]{2,0,1:T(8,128)S(1)} %add.110), channel_id=1, source_target_pairs={{480,0},{0,32},{32,64},{64,96},{96,128},{128,160},{160,192},{192,2... | collective-permute-start | bytes 393224 | tf_op jit(solution)/shard_map/while/body/eval_jaxpr/ppermute | solution.py:22
  278.6 5.4 %collective-permute-start.1 = (bf16[128,2,128]{2,0,1:T(8,128)(2,1)}, bf16[128,2,128]{2,0,1:T(8,128)(2,1)S(1)}, u32[]{:S(2)}, u32[]{:S(2)}) collective-permute-start(bf16[128,2,128]{2,0,1:T(8,128)(2,1)} %copy.107), channel_id=1, source_target_pairs={{0,32},{32,64},{64,96},{96,128},{128,160},{160,192},{192,224},{224... | collective-permute-start | bytes 196616 | tf_op jit(solution)/shard_map/while/body/eval_jaxpr/ppermute | solution.py:16
  286.1 6.3 %collective-permute-start.3 = (f32[128,2,128]{2,0,1:T(8,128)S(1)}, f32[128,2,128]{2,0,1:T(8,128)S(1)}, u32[]{:S(2)}, u32[]{:S(2)}) collective-permute-start(f32[128,2,128]{2,0,1:T(8,128)S(1)} %add.110), channel_id=1, source_target_pairs={{480,0},{0,32},{32,64},{64,96},{96,128},{128,160},{160,192},{192,2... | collective-permute-start | bytes 393224 | tf_op jit(solution)/shard_map/while/body/eval_jaxpr/ppermute | solution.py:22
  292.6 3.6 collective-permute-done.3
  298.8 4.8 collective-permute-start.1
  308.8 7.0 %collective-permute-done.3 = f32[128,2,128]{2,0,1:T(8,128)S(1)} collective-permute-done((f32[128,2,128]{2,0,1:T(8,128)S(1)}, f32[128,2,128]{2,0,1:T(8,128)S(1)}, u32[]{:S(2)}, u32[]{:S(2)}) %collective-permute-start.3) | collective-permute-done | bytes 131104 | tf_op jit(solution)/shard_map/while/body/eval_jaxpr/ppermute | solution.py:22
  321.9 6.5 %collective-permute-start.3 = (f32[128,2,128]{2,0,1:T(8,128)S(1)}, f32[128,2,128]{2,0,1:T(8,128)S(1)}, u32[]{:S(2)}, u32[]{:S(2)}) collective-permute-start(f32[128,2,128]{2,0,1:T(8,128)S(1)} %add.110), channel_id=1, source_target_pairs={{480,0},{0,32},{32,64},{64,96},{96,128},{128,160},{160,192},{192,2... | collective-permute-start | bytes 393224 | tf_op jit(solution)/shard_map/while/body/eval_jaxpr/ppermute | solution.py:22
  334.5 5.0 %collective-permute-start.1 = (bf16[128,2,128]{2,0,1:T(8,128)(2,1)}, bf16[128,2,128]{2,0,1:T(8,128)(2,1)S(1)}, u32[]{:S(2)}, u32[]{:S(2)}) collective-permute-start(bf16[128,2,128]{2,0,1:T(8,128)(2,1)} %copy.107), channel_id=1, source_target_pairs={{0,32},{32,64},{64,96},{96,128},{128,160},{160,192},{192,224},{224... | collective-permute-start | bytes 196616 | tf_op jit(solution)/shard_map/while/body/eval_jaxpr/ppermute | solution.py:16
  341.6 6.3 %collective-permute-start.3 = (f32[128,2,128]{2,0,1:T(8,128)S(1)}, f32[128,2,128]{2,0,1:T(8,128)S(1)}, u32[]{:S(2)}, u32[]{:S(2)}) collective-permute-start(f32[128,2,128]{2,0,1:T(8,128)S(1)} %add.110), channel_id=1, source_target_pairs={{480,0},{0,32},{32,64},{64,96},{96,128},{128,160},{160,192},{192,2... | collective-permute-start | bytes 393224 | tf_op jit(solution)/shard_map/while/body/eval_jaxpr/ppermute | solution.py:22
  348.1 3.6 collective-permute-done.3
  354.2 4.8 collective-permute-start.1
  361.2 5.2 %collective-permute-start.3 = (f32[128,2,128]{2,0,1:T(8,128)S(1)}, f32[128,2,128]{2,0,1:T(8,128)S(1)}, u32[]{:S(2)}, u32[]{:S(2)}) collective-permute-start(f32[128,2,128]{2,0,1:T(8,128)S(1)} %add.110), channel_id=1, source_target_pairs={{480,0},{0,32},{32,64},{64,96},{96,128},{128,160},{160,192},{192,2... | collective-permute-start | bytes 393224 | tf_op jit(solution)/shard_map/while/body/eval_jaxpr/ppermute | solution.py:22
  366.5 4.7 collective-permute-done.3
  373.8 3.7 collective-permute-start.1
  379.6 6.5 %collective-permute-start.3 = (f32[128,2,128]{2,0,1:T(8,128)S(1)}, f32[128,2,128]{2,0,1:T(8,128)S(1)}, u32[]{:S(2)}, u32[]{:S(2)}) collective-permute-start(f32[128,2,128]{2,0,1:T(8,128)S(1)} %add.110), channel_id=1, source_target_pairs={{480,0},{0,32},{32,64},{64,96},{96,128},{128,160},{160,192},{192,2... | collective-permute-start | bytes 393224 | tf_op jit(solution)/shard_map/while/body/eval_jaxpr/ppermute | solution.py:22
  392.3 5.0 %collective-permute-start.1 = (bf16[128,2,128]{2,0,1:T(8,128)(2,1)}, bf16[128,2,128]{2,0,1:T(8,128)(2,1)S(1)}, u32[]{:S(2)}, u32[]{:S(2)}) collective-permute-start(bf16[128,2,128]{2,0,1:T(8,128)(2,1)} %copy.107), channel_id=1, source_target_pairs={{0,32},{32,64},{64,96},{96,128},{128,160},{160,192},{192,224},{224... | collective-permute-start | bytes 196616 | tf_op jit(solution)/shard_map/while/body/eval_jaxpr/ppermute | solution.py:16
  399.4 6.3 %collective-permute-start.3 = (f32[128,2,128]{2,0,1:T(8,128)S(1)}, f32[128,2,128]{2,0,1:T(8,128)S(1)}, u32[]{:S(2)}, u32[]{:S(2)}) collective-permute-start(f32[128,2,128]{2,0,1:T(8,128)S(1)} %add.110), channel_id=1, source_target_pairs={{480,0},{0,32},{32,64},{64,96},{96,128},{128,160},{160,192},{192,2... | collective-permute-start | bytes 393224 | tf_op jit(solution)/shard_map/while/body/eval_jaxpr/ppermute | solution.py:22
  405.8 3.6 collective-permute-done.3
  412.0 4.8 collective-permute-start.1
  422.0 7.0 %collective-permute-done.3 = f32[128,2,128]{2,0,1:T(8,128)S(1)} collective-permute-done((f32[128,2,128]{2,0,1:T(8,128)S(1)}, f32[128,2,128]{2,0,1:T(8,128)S(1)}, u32[]{:S(2)}, u32[]{:S(2)}) %collective-permute-start.3) | collective-permute-done | bytes 131104 | tf_op jit(solution)/shard_map/while/body/eval_jaxpr/ppermute | solution.py:22
  435.1 6.5 %collective-permute-start.3 = (f32[128,2,128]{2,0,1:T(8,128)S(1)}, f32[128,2,128]{2,0,1:T(8,128)S(1)}, u32[]{:S(2)}, u32[]{:S(2)}) collective-permute-start(f32[128,2,128]{2,0,1:T(8,128)S(1)} %add.110), channel_id=1, source_target_pairs={{480,0},{0,32},{32,64},{64,96},{96,128},{128,160},{160,192},{192,2... | collective-permute-start | bytes 393224 | tf_op jit(solution)/shard_map/while/body/eval_jaxpr/ppermute | solution.py:22
  447.8 5.0 %collective-permute-start.1 = (bf16[128,2,128]{2,0,1:T(8,128)(2,1)}, bf16[128,2,128]{2,0,1:T(8,128)(2,1)S(1)}, u32[]{:S(2)}, u32[]{:S(2)}) collective-permute-start(bf16[128,2,128]{2,0,1:T(8,128)(2,1)} %copy.107), channel_id=1, source_target_pairs={{0,32},{32,64},{64,96},{96,128},{128,160},{160,192},{192,224},{224... | collective-permute-start | bytes 196616 | tf_op jit(solution)/shard_map/while/body/eval_jaxpr/ppermute | solution.py:16
  454.8 6.3 %collective-permute-start.3 = (f32[128,2,128]{2,0,1:T(8,128)S(1)}, f32[128,2,128]{2,0,1:T(8,128)S(1)}, u32[]{:S(2)}, u32[]{:S(2)}) collective-permute-start(f32[128,2,128]{2,0,1:T(8,128)S(1)} %add.110), channel_id=1, source_target_pairs={{480,0},{0,32},{32,64},{64,96},{96,128},{128,160},{160,192},{192,2... | collective-permute-start | bytes 393224 | tf_op jit(solution)/shard_map/while/body/eval_jaxpr/ppermute | solution.py:22
  461.3 3.6 collective-permute-done.3
  467.1 6.8 %reshape.127 = bf16[7168,1,1,64]{3,2,1,0:T(2,128)(2,1)} reshape(bf16[16,2,14336]{2,1,0:T(2,128)(2,1)S(1)} %all-to-all-done.1) | data formatting | bytes 1835008
  473.9 7.2 %copy.82 = bf16[1,1,64,7168]{3,2,1,0:T(8,128)(2,1)S(1)} copy(bf16[1,1,64,7168]{2,1,0,3:T(2,128)(2,1)} %bitcast.83) | data formatting | bytes 1835008 | tf_op jit(solution)/shard_map/all_to_all | solution.py:113
  483.0 5.5 %fusion.15 = bf16[1,2048,448]{1,2,0:T(8,128)(2,1)} fusion(bf16[1024,448]{1,0:T(8,128)(2,1)S(1)} %bitcast.88, bf16[1,1024,2048]{2,1,0:T(8,128)(2,1)} %all-gather.2.cloned.1.call-done), kind=kOutput, calls=%fused_computation.23 | convolution fusion | flops 1879965696 | bytes 6946816 | tf_op jit(solution)/shard_map/esf,esd->efd/dot_general | solution.py:122
  (296 shorter events, 131.8 us)
Async XLA Ops:
  7.2 475.8 %all-gather.2.cloned.1.call-start = ((), (), s32[]{:S(2)}) async-start(), calls=%async_computation.2 | async-start | bytes 4456448 | tf_op jit(solution)/shard_map/all_gather | solution.py:124
  23.6 70.8 %all-to-all-start = ((bf16[32,1,64,224]{3,2,1,0:T(8,128)(2,1)}), bf16[32,1,64,224]{3,2,1,0:T(8,128)(2,1)S(1)}, u32[]{:S(2)}, u32[]{:S(2)}) async-start(bf16[32,1,64,224]{3,2,1,0:T(8,128)(2,1)} %bitcast.15), calls=%async_computation | async-start | bytes 2097152 | tf_op jit(solution)/shard_map/all_to_all | solution.py:114
  143.1 323.9 %all-to-all-start.1 = ((bf16[16,2,14336]{2,1,0:T(2,128)(2,1)}), bf16[16,2,14336]{2,1,0:T(2,128)(2,1)S(1)}, u32[]{:S(2)}, u32[]{:S(2)}) async-start(bf16[16,2,14336]{2,1,0:T(2,128)(2,1)} %reshape.126), calls=%async_computation.1 | async-start | bytes 1835008 | tf_op jit(solution)/shard_map/all_to_all | solution.py:113
  150.6 17.3 %collective-permute-start = (bf16[128,2,192]{0,2,1:T(8,128)(2,1)}, bf16[128,2,192]{0,2,1:T(8,128)(2,1)S(1)}, u32[]{:S(2)}, u32[]{:S(2)}) collective-permute-start(bf16[128,2,192]{0,2,1:T(8,128)(2,1)} %copy.106), channel_id=1, source_target_pairs={{0,32},{32,64},{64,96},{96,128},{128,160},{160,192},{192,224},{224... | collective-permute-start | bytes 294920 | tf_op jit(solution)/shard_map/while/body/eval_jaxpr/ppermute | solution.py:16
  153.6 14.4 %collective-permute-start.1 = (bf16[128,2,128]{2,0,1:T(8,128)(2,1)}, bf16[128,2,128]{2,0,1:T(8,128)(2,1)S(1)}, u32[]{:S(2)}, u32[]{:S(2)}) collective-permute-start(bf16[128,2,128]{2,0,1:T(8,128)(2,1)} %copy.107), channel_id=1, source_target_pairs={{0,32},{32,64},{64,96},{96,128},{128,160},{160,192},{192,224},{224... | collective-permute-start | bytes 196616 | tf_op jit(solution)/shard_map/while/body/eval_jaxpr/ppermute | solution.py:16
  162.4 12.0 %collective-permute-start.2 = (f32[128,2,192]{0,2,1:T(8,128)S(1)}, f32[128,2,192]{0,2,1:T(8,128)S(1)}, u32[]{:S(2)}, u32[]{:S(2)}) collective-permute-start(f32[128,2,192]{0,2,1:T(8,128)S(1)} %add.109), channel_id=1, source_target_pairs={{480,0},{0,32},{32,64},{64,96},{96,128},{128,160},{160,192},{192,2... | collective-permute-start | bytes 589832 | tf_op jit(solution)/shard_map/while/body/eval_jaxpr/ppermute | solution.py:22
  175.1 15.6 %collective-permute-start = (bf16[128,2,192]{0,2,1:T(8,128)(2,1)}, bf16[128,2,192]{0,2,1:T(8,128)(2,1)S(1)}, u32[]{:S(2)}, u32[]{:S(2)}) collective-permute-start(bf16[128,2,192]{0,2,1:T(8,128)(2,1)} %copy.106), channel_id=1, source_target_pairs={{0,32},{32,64},{64,96},{96,128},{128,160},{160,192},{192,224},{224... | collective-permute-start | bytes 294920 | tf_op jit(solution)/shard_map/while/body/eval_jaxpr/ppermute | solution.py:16
  177.0 13.7 %collective-permute-start.1 = (bf16[128,2,128]{2,0,1:T(8,128)(2,1)}, bf16[128,2,128]{2,0,1:T(8,128)(2,1)S(1)}, u32[]{:S(2)}, u32[]{:S(2)}) collective-permute-start(bf16[128,2,128]{2,0,1:T(8,128)(2,1)} %copy.107), channel_id=1, source_target_pairs={{0,32},{32,64},{64,96},{96,128},{128,160},{160,192},{192,224},{224... | collective-permute-start | bytes 196616 | tf_op jit(solution)/shard_map/while/body/eval_jaxpr/ppermute | solution.py:16
  179.1 15.5 %collective-permute-start.2 = (f32[128,2,192]{0,2,1:T(8,128)S(1)}, f32[128,2,192]{0,2,1:T(8,128)S(1)}, u32[]{:S(2)}, u32[]{:S(2)}) collective-permute-start(f32[128,2,192]{0,2,1:T(8,128)S(1)} %add.109), channel_id=1, source_target_pairs={{480,0},{0,32},{32,64},{64,96},{96,128},{128,160},{160,192},{192,2... | collective-permute-start | bytes 589832 | tf_op jit(solution)/shard_map/while/body/eval_jaxpr/ppermute | solution.py:22
  195.3 15.8 %collective-permute-start = (bf16[128,2,192]{0,2,1:T(8,128)(2,1)}, bf16[128,2,192]{0,2,1:T(8,128)(2,1)S(1)}, u32[]{:S(2)}, u32[]{:S(2)}) collective-permute-start(bf16[128,2,192]{0,2,1:T(8,128)(2,1)} %copy.106), channel_id=1, source_target_pairs={{0,32},{32,64},{64,96},{96,128},{128,160},{160,192},{192,224},{224... | collective-permute-start | bytes 294920 | tf_op jit(solution)/shard_map/while/body/eval_jaxpr/ppermute | solution.py:16
  197.2 13.9 %collective-permute-start.1 = (bf16[128,2,128]{2,0,1:T(8,128)(2,1)}, bf16[128,2,128]{2,0,1:T(8,128)(2,1)S(1)}, u32[]{:S(2)}, u32[]{:S(2)}) collective-permute-start(bf16[128,2,128]{2,0,1:T(8,128)(2,1)} %copy.107), channel_id=1, source_target_pairs={{0,32},{32,64},{64,96},{96,128},{128,160},{160,192},{192,224},{224... | collective-permute-start | bytes 196616 | tf_op jit(solution)/shard_map/while/body/eval_jaxpr/ppermute | solution.py:16
  201.9 12.0 %collective-permute-start.2 = (f32[128,2,192]{0,2,1:T(8,128)S(1)}, f32[128,2,192]{0,2,1:T(8,128)S(1)}, u32[]{:S(2)}, u32[]{:S(2)}) collective-permute-start(f32[128,2,192]{0,2,1:T(8,128)S(1)} %add.109), channel_id=1, source_target_pairs={{480,0},{0,32},{32,64},{64,96},{96,128},{128,160},{160,192},{192,2... | collective-permute-start | bytes 589832 | tf_op jit(solution)/shard_map/while/body/eval_jaxpr/ppermute | solution.py:22
  214.5 15.6 %collective-permute-start = (bf16[128,2,192]{0,2,1:T(8,128)(2,1)}, bf16[128,2,192]{0,2,1:T(8,128)(2,1)S(1)}, u32[]{:S(2)}, u32[]{:S(2)}) collective-permute-start(bf16[128,2,192]{0,2,1:T(8,128)(2,1)} %copy.106), channel_id=1, source_target_pairs={{0,32},{32,64},{64,96},{96,128},{128,160},{160,192},{192,224},{224... | collective-permute-start | bytes 294920 | tf_op jit(solution)/shard_map/while/body/eval_jaxpr/ppermute | solution.py:16
  216.5 13.7 %collective-permute-start.1 = (bf16[128,2,128]{2,0,1:T(8,128)(2,1)}, bf16[128,2,128]{2,0,1:T(8,128)(2,1)S(1)}, u32[]{:S(2)}, u32[]{:S(2)}) collective-permute-start(bf16[128,2,128]{2,0,1:T(8,128)(2,1)} %copy.107), channel_id=1, source_target_pairs={{0,32},{32,64},{64,96},{96,128},{128,160},{160,192},{192,224},{224... | collective-permute-start | bytes 196616 | tf_op jit(solution)/shard_map/while/body/eval_jaxpr/ppermute | solution.py:16
  222.2 12.0 %collective-permute-start.2 = (f32[128,2,192]{0,2,1:T(8,128)S(1)}, f32[128,2,192]{0,2,1:T(8,128)S(1)}, u32[]{:S(2)}, u32[]{:S(2)}) collective-permute-start(f32[128,2,192]{0,2,1:T(8,128)S(1)} %add.109), channel_id=1, source_target_pairs={{480,0},{0,32},{32,64},{64,96},{96,128},{128,160},{160,192},{192,2... | collective-permute-start | bytes 589832 | tf_op jit(solution)/shard_map/while/body/eval_jaxpr/ppermute | solution.py:22
  234.9 15.3 %collective-permute-start = (bf16[128,2,192]{0,2,1:T(8,128)(2,1)}, bf16[128,2,192]{0,2,1:T(8,128)(2,1)S(1)}, u32[]{:S(2)}, u32[]{:S(2)}) collective-permute-start(bf16[128,2,192]{0,2,1:T(8,128)(2,1)} %copy.106), channel_id=1, source_target_pairs={{0,32},{32,64},{64,96},{96,128},{128,160},{160,192},{192,224},{224... | collective-permute-start | bytes 294920 | tf_op jit(solution)/shard_map/while/body/eval_jaxpr/ppermute | solution.py:16
  238.9 11.4 %collective-permute-start.1 = (bf16[128,2,128]{2,0,1:T(8,128)(2,1)}, bf16[128,2,128]{2,0,1:T(8,128)(2,1)S(1)}, u32[]{:S(2)}, u32[]{:S(2)}) collective-permute-start(bf16[128,2,128]{2,0,1:T(8,128)(2,1)} %copy.107), channel_id=1, source_target_pairs={{0,32},{32,64},{64,96},{96,128},{128,160},{160,192},{192,224},{224... | collective-permute-start | bytes 196616 | tf_op jit(solution)/shard_map/while/body/eval_jaxpr/ppermute | solution.py:16
  244.9 12.0 %collective-permute-start.2 = (f32[128,2,192]{0,2,1:T(8,128)S(1)}, f32[128,2,192]{0,2,1:T(8,128)S(1)}, u32[]{:S(2)}, u32[]{:S(2)}) collective-permute-start(f32[128,2,192]{0,2,1:T(8,128)S(1)} %add.109), channel_id=1, source_target_pairs={{480,0},{0,32},{32,64},{64,96},{96,128},{128,160},{160,192},{192,2... | collective-permute-start | bytes 589832 | tf_op jit(solution)/shard_map/while/body/eval_jaxpr/ppermute | solution.py:22
  257.5 15.5 %collective-permute-start = (bf16[128,2,192]{0,2,1:T(8,128)(2,1)}, bf16[128,2,192]{0,2,1:T(8,128)(2,1)S(1)}, u32[]{:S(2)}, u32[]{:S(2)}) collective-permute-start(bf16[128,2,192]{0,2,1:T(8,128)(2,1)} %copy.106), channel_id=1, source_target_pairs={{0,32},{32,64},{64,96},{96,128},{128,160},{160,192},{192,224},{224... | collective-permute-start | bytes 294920 | tf_op jit(solution)/shard_map/while/body/eval_jaxpr/ppermute | solution.py:16
  259.4 13.6 %collective-permute-start.1 = (bf16[128,2,128]{2,0,1:T(8,128)(2,1)}, bf16[128,2,128]{2,0,1:T(8,128)(2,1)S(1)}, u32[]{:S(2)}, u32[]{:S(2)}) collective-permute-start(bf16[128,2,128]{2,0,1:T(8,128)(2,1)} %copy.107), channel_id=1, source_target_pairs={{0,32},{32,64},{64,96},{96,128},{128,160},{160,192},{192,224},{224... | collective-permute-start | bytes 196616 | tf_op jit(solution)/shard_map/while/body/eval_jaxpr/ppermute | solution.py:16
  263.1 12.9 %collective-permute-start.2 = (f32[128,2,192]{0,2,1:T(8,128)S(1)}, f32[128,2,192]{0,2,1:T(8,128)S(1)}, u32[]{:S(2)}, u32[]{:S(2)}) collective-permute-start(f32[128,2,192]{0,2,1:T(8,128)S(1)} %add.109), channel_id=1, source_target_pairs={{480,0},{0,32},{32,64},{64,96},{96,128},{128,160},{160,192},{192,2... | collective-permute-start | bytes 589832 | tf_op jit(solution)/shard_map/while/body/eval_jaxpr/ppermute | solution.py:22
  276.7 15.9 %collective-permute-start = (bf16[128,2,192]{0,2,1:T(8,128)(2,1)}, bf16[128,2,192]{0,2,1:T(8,128)(2,1)S(1)}, u32[]{:S(2)}, u32[]{:S(2)}) collective-permute-start(bf16[128,2,192]{0,2,1:T(8,128)(2,1)} %copy.106), channel_id=1, source_target_pairs={{0,32},{32,64},{64,96},{96,128},{128,160},{160,192},{192,224},{224... | collective-permute-start | bytes 294920 | tf_op jit(solution)/shard_map/while/body/eval_jaxpr/ppermute | solution.py:16
  278.6 14.0 %collective-permute-start.1 = (bf16[128,2,128]{2,0,1:T(8,128)(2,1)}, bf16[128,2,128]{2,0,1:T(8,128)(2,1)S(1)}, u32[]{:S(2)}, u32[]{:S(2)}) collective-permute-start(bf16[128,2,128]{2,0,1:T(8,128)(2,1)} %copy.107), channel_id=1, source_target_pairs={{0,32},{32,64},{64,96},{96,128},{128,160},{160,192},{192,224},{224... | collective-permute-start | bytes 196616 | tf_op jit(solution)/shard_map/while/body/eval_jaxpr/ppermute | solution.py:16
  284.2 12.0 %collective-permute-start.2 = (f32[128,2,192]{0,2,1:T(8,128)S(1)}, f32[128,2,192]{0,2,1:T(8,128)S(1)}, u32[]{:S(2)}, u32[]{:S(2)}) collective-permute-start(f32[128,2,192]{0,2,1:T(8,128)S(1)} %add.109), channel_id=1, source_target_pairs={{480,0},{0,32},{32,64},{64,96},{96,128},{128,160},{160,192},{192,2... | collective-permute-start | bytes 589832 | tf_op jit(solution)/shard_map/while/body/eval_jaxpr/ppermute | solution.py:22
  296.8 11.9 %collective-permute-start = (bf16[128,2,192]{0,2,1:T(8,128)(2,1)}, bf16[128,2,192]{0,2,1:T(8,128)(2,1)S(1)}, u32[]{:S(2)}, u32[]{:S(2)}) collective-permute-start(bf16[128,2,192]{0,2,1:T(8,128)(2,1)} %copy.106), channel_id=1, source_target_pairs={{0,32},{32,64},{64,96},{96,128},{128,160},{160,192},{192,224},{224... | collective-permute-start | bytes 294920 | tf_op jit(solution)/shard_map/while/body/eval_jaxpr/ppermute | solution.py:16
  303.7 12.0 %collective-permute-start.2 = (f32[128,2,192]{0,2,1:T(8,128)S(1)}, f32[128,2,192]{0,2,1:T(8,128)S(1)}, u32[]{:S(2)}, u32[]{:S(2)}) collective-permute-start(f32[128,2,192]{0,2,1:T(8,128)S(1)} %add.109), channel_id=1, source_target_pairs={{480,0},{0,32},{32,64},{64,96},{96,128},{128,160},{160,192},{192,2... | collective-permute-start | bytes 589832 | tf_op jit(solution)/shard_map/while/body/eval_jaxpr/ppermute | solution.py:22
  316.4 12.1 %collective-permute-start = (bf16[128,2,192]{0,2,1:T(8,128)(2,1)}, bf16[128,2,192]{0,2,1:T(8,128)(2,1)S(1)}, u32[]{:S(2)}, u32[]{:S(2)}) collective-permute-start(bf16[128,2,192]{0,2,1:T(8,128)(2,1)} %copy.106), channel_id=1, source_target_pairs={{0,32},{32,64},{64,96},{96,128},{128,160},{160,192},{192,224},{224... | collective-permute-start | bytes 294920 | tf_op jit(solution)/shard_map/while/body/eval_jaxpr/ppermute | solution.py:16
  318.3 10.2 %collective-permute-start.1 = (bf16[128,2,128]{2,0,1:T(8,128)(2,1)}, bf16[128,2,128]{2,0,1:T(8,128)(2,1)S(1)}, u32[]{:S(2)}, u32[]{:S(2)}) collective-permute-start(bf16[128,2,128]{2,0,1:T(8,128)(2,1)} %copy.107), channel_id=1, source_target_pairs={{0,32},{32,64},{64,96},{96,128},{128,160},{160,192},{192,224},{224... | collective-permute-start | bytes 196616 | tf_op jit(solution)/shard_map/while/body/eval_jaxpr/ppermute | solution.py:16
  319.9 12.0 %collective-permute-start.2 = (f32[128,2,192]{0,2,1:T(8,128)S(1)}, f32[128,2,192]{0,2,1:T(8,128)S(1)}, u32[]{:S(2)}, u32[]{:S(2)}) collective-permute-start(f32[128,2,192]{0,2,1:T(8,128)S(1)} %add.109), channel_id=1, source_target_pairs={{480,0},{0,32},{32,64},{64,96},{96,128},{128,160},{160,192},{192,2... | collective-permute-start | bytes 589832 | tf_op jit(solution)/shard_map/while/body/eval_jaxpr/ppermute | solution.py:22
  332.6 15.4 %collective-permute-start = (bf16[128,2,192]{0,2,1:T(8,128)(2,1)}, bf16[128,2,192]{0,2,1:T(8,128)(2,1)S(1)}, u32[]{:S(2)}, u32[]{:S(2)}) collective-permute-start(bf16[128,2,192]{0,2,1:T(8,128)(2,1)} %copy.106), channel_id=1, source_target_pairs={{0,32},{32,64},{64,96},{96,128},{128,160},{160,192},{192,224},{224... | collective-permute-start | bytes 294920 | tf_op jit(solution)/shard_map/while/body/eval_jaxpr/ppermute | solution.py:16
  334.5 13.5 %collective-permute-start.1 = (bf16[128,2,128]{2,0,1:T(8,128)(2,1)}, bf16[128,2,128]{2,0,1:T(8,128)(2,1)S(1)}, u32[]{:S(2)}, u32[]{:S(2)}) collective-permute-start(bf16[128,2,128]{2,0,1:T(8,128)(2,1)} %copy.107), channel_id=1, source_target_pairs={{0,32},{32,64},{64,96},{96,128},{128,160},{160,192},{192,224},{224... | collective-permute-start | bytes 196616 | tf_op jit(solution)/shard_map/while/body/eval_jaxpr/ppermute | solution.py:16
  339.7 12.0 %collective-permute-start.2 = (f32[128,2,192]{0,2,1:T(8,128)S(1)}, f32[128,2,192]{0,2,1:T(8,128)S(1)}, u32[]{:S(2)}, u32[]{:S(2)}) collective-permute-start(f32[128,2,192]{0,2,1:T(8,128)S(1)} %add.109), channel_id=1, source_target_pairs={{480,0},{0,32},{32,64},{64,96},{96,128},{128,160},{160,192},{192,2... | collective-permute-start | bytes 589832 | tf_op jit(solution)/shard_map/while/body/eval_jaxpr/ppermute | solution.py:22
  352.3 14.2 %collective-permute-start = (bf16[128,2,192]{0,2,1:T(8,128)(2,1)}, bf16[128,2,192]{0,2,1:T(8,128)(2,1)S(1)}, u32[]{:S(2)}, u32[]{:S(2)}) collective-permute-start(bf16[128,2,192]{0,2,1:T(8,128)(2,1)} %copy.106), channel_id=1, source_target_pairs={{0,32},{32,64},{64,96},{96,128},{128,160},{160,192},{192,224},{224... | collective-permute-start | bytes 294920 | tf_op jit(solution)/shard_map/while/body/eval_jaxpr/ppermute | solution.py:16
  354.2 12.3 %collective-permute-start.1 = (bf16[128,2,128]{2,0,1:T(8,128)(2,1)}, bf16[128,2,128]{2,0,1:T(8,128)(2,1)S(1)}, u32[]{:S(2)}, u32[]{:S(2)}) collective-permute-start(bf16[128,2,128]{2,0,1:T(8,128)(2,1)} %copy.107), channel_id=1, source_target_pairs={{0,32},{32,64},{64,96},{96,128},{128,160},{160,192},{192,224},{224... | collective-permute-start | bytes 196616 | tf_op jit(solution)/shard_map/while/body/eval_jaxpr/ppermute | solution.py:16
  359.2 12.0 %collective-permute-start.2 = (f32[128,2,192]{0,2,1:T(8,128)S(1)}, f32[128,2,192]{0,2,1:T(8,128)S(1)}, u32[]{:S(2)}, u32[]{:S(2)}) collective-permute-start(f32[128,2,192]{0,2,1:T(8,128)S(1)} %add.109), channel_id=1, source_target_pairs={{480,0},{0,32},{32,64},{64,96},{96,128},{128,160},{160,192},{192,2... | collective-permute-start | bytes 589832 | tf_op jit(solution)/shard_map/while/body/eval_jaxpr/ppermute | solution.py:22
  371.9 14.4 %collective-permute-start = (bf16[128,2,192]{0,2,1:T(8,128)(2,1)}, bf16[128,2,192]{0,2,1:T(8,128)(2,1)S(1)}, u32[]{:S(2)}, u32[]{:S(2)}) collective-permute-start(bf16[128,2,192]{0,2,1:T(8,128)(2,1)} %copy.106), channel_id=1, source_target_pairs={{0,32},{32,64},{64,96},{96,128},{128,160},{160,192},{192,224},{224... | collective-permute-start | bytes 294920 | tf_op jit(solution)/shard_map/while/body/eval_jaxpr/ppermute | solution.py:16
  373.8 12.4 %collective-permute-start.1 = (bf16[128,2,128]{2,0,1:T(8,128)(2,1)}, bf16[128,2,128]{2,0,1:T(8,128)(2,1)S(1)}, u32[]{:S(2)}, u32[]{:S(2)}) collective-permute-start(bf16[128,2,128]{2,0,1:T(8,128)(2,1)} %copy.107), channel_id=1, source_target_pairs={{0,32},{32,64},{64,96},{96,128},{128,160},{160,192},{192,224},{224... | collective-permute-start | bytes 196616 | tf_op jit(solution)/shard_map/while/body/eval_jaxpr/ppermute | solution.py:16
  377.7 12.0 %collective-permute-start.2 = (f32[128,2,192]{0,2,1:T(8,128)S(1)}, f32[128,2,192]{0,2,1:T(8,128)S(1)}, u32[]{:S(2)}, u32[]{:S(2)}) collective-permute-start(f32[128,2,192]{0,2,1:T(8,128)S(1)} %add.109), channel_id=1, source_target_pairs={{480,0},{0,32},{32,64},{64,96},{96,128},{128,160},{160,192},{192,2... | collective-permute-start | bytes 589832 | tf_op jit(solution)/shard_map/while/body/eval_jaxpr/ppermute | solution.py:22
  390.3 15.5 %collective-permute-start = (bf16[128,2,192]{0,2,1:T(8,128)(2,1)}, bf16[128,2,192]{0,2,1:T(8,128)(2,1)S(1)}, u32[]{:S(2)}, u32[]{:S(2)}) collective-permute-start(bf16[128,2,192]{0,2,1:T(8,128)(2,1)} %copy.106), channel_id=1, source_target_pairs={{0,32},{32,64},{64,96},{96,128},{128,160},{160,192},{192,224},{224... | collective-permute-start | bytes 294920 | tf_op jit(solution)/shard_map/while/body/eval_jaxpr/ppermute | solution.py:16
  392.3 13.5 %collective-permute-start.1 = (bf16[128,2,128]{2,0,1:T(8,128)(2,1)}, bf16[128,2,128]{2,0,1:T(8,128)(2,1)S(1)}, u32[]{:S(2)}, u32[]{:S(2)}) collective-permute-start(bf16[128,2,128]{2,0,1:T(8,128)(2,1)} %copy.107), channel_id=1, source_target_pairs={{0,32},{32,64},{64,96},{96,128},{128,160},{160,192},{192,224},{224... | collective-permute-start | bytes 196616 | tf_op jit(solution)/shard_map/while/body/eval_jaxpr/ppermute | solution.py:16
  397.4 12.0 %collective-permute-start.2 = (f32[128,2,192]{0,2,1:T(8,128)S(1)}, f32[128,2,192]{0,2,1:T(8,128)S(1)}, u32[]{:S(2)}, u32[]{:S(2)}) collective-permute-start(f32[128,2,192]{0,2,1:T(8,128)S(1)} %add.109), channel_id=1, source_target_pairs={{480,0},{0,32},{32,64},{64,96},{96,128},{128,160},{160,192},{192,2... | collective-permute-start | bytes 589832 | tf_op jit(solution)/shard_map/while/body/eval_jaxpr/ppermute | solution.py:22
  410.1 11.9 %collective-permute-start = (bf16[128,2,192]{0,2,1:T(8,128)(2,1)}, bf16[128,2,192]{0,2,1:T(8,128)(2,1)S(1)}, u32[]{:S(2)}, u32[]{:S(2)}) collective-permute-start(bf16[128,2,192]{0,2,1:T(8,128)(2,1)} %copy.106), channel_id=1, source_target_pairs={{0,32},{32,64},{64,96},{96,128},{128,160},{160,192},{192,224},{224... | collective-permute-start | bytes 294920 | tf_op jit(solution)/shard_map/while/body/eval_jaxpr/ppermute | solution.py:16
  417.0 12.0 %collective-permute-start.2 = (f32[128,2,192]{0,2,1:T(8,128)S(1)}, f32[128,2,192]{0,2,1:T(8,128)S(1)}, u32[]{:S(2)}, u32[]{:S(2)}) collective-permute-start(f32[128,2,192]{0,2,1:T(8,128)S(1)} %add.109), channel_id=1, source_target_pairs={{480,0},{0,32},{32,64},{64,96},{96,128},{128,160},{160,192},{192,2... | collective-permute-start | bytes 589832 | tf_op jit(solution)/shard_map/while/body/eval_jaxpr/ppermute | solution.py:22
  429.6 12.1 %collective-permute-start = (bf16[128,2,192]{0,2,1:T(8,128)(2,1)}, bf16[128,2,192]{0,2,1:T(8,128)(2,1)S(1)}, u32[]{:S(2)}, u32[]{:S(2)}) collective-permute-start(bf16[128,2,192]{0,2,1:T(8,128)(2,1)} %copy.106), channel_id=1, source_target_pairs={{0,32},{32,64},{64,96},{96,128},{128,160},{160,192},{192,224},{224... | collective-permute-start | bytes 294920 | tf_op jit(solution)/shard_map/while/body/eval_jaxpr/ppermute | solution.py:16
  433.2 12.0 %collective-permute-start.2 = (f32[128,2,192]{0,2,1:T(8,128)S(1)}, f32[128,2,192]{0,2,1:T(8,128)S(1)}, u32[]{:S(2)}, u32[]{:S(2)}) collective-permute-start(f32[128,2,192]{0,2,1:T(8,128)S(1)} %add.109), channel_id=1, source_target_pairs={{480,0},{0,32},{32,64},{64,96},{96,128},{128,160},{160,192},{192,2... | collective-permute-start | bytes 589832 | tf_op jit(solution)/shard_map/while/body/eval_jaxpr/ppermute | solution.py:22
  445.8 15.4 %collective-permute-start = (bf16[128,2,192]{0,2,1:T(8,128)(2,1)}, bf16[128,2,192]{0,2,1:T(8,128)(2,1)S(1)}, u32[]{:S(2)}, u32[]{:S(2)}) collective-permute-start(bf16[128,2,192]{0,2,1:T(8,128)(2,1)} %copy.106), channel_id=1, source_target_pairs={{0,32},{32,64},{64,96},{96,128},{128,160},{160,192},{192,224},{224... | collective-permute-start | bytes 294920 | tf_op jit(solution)/shard_map/while/body/eval_jaxpr/ppermute | solution.py:16
  447.8 13.5 %collective-permute-start.1 = (bf16[128,2,128]{2,0,1:T(8,128)(2,1)}, bf16[128,2,128]{2,0,1:T(8,128)(2,1)S(1)}, u32[]{:S(2)}, u32[]{:S(2)}) collective-permute-start(bf16[128,2,128]{2,0,1:T(8,128)(2,1)} %copy.107), channel_id=1, source_target_pairs={{0,32},{32,64},{64,96},{96,128},{128,160},{160,192},{192,224},{224... | collective-permute-start | bytes 196616 | tf_op jit(solution)/shard_map/while/body/eval_jaxpr/ppermute | solution.py:16
  452.9 12.0 %collective-permute-start.2 = (f32[128,2,192]{0,2,1:T(8,128)S(1)}, f32[128,2,192]{0,2,1:T(8,128)S(1)}, u32[]{:S(2)}, u32[]{:S(2)}) collective-permute-start(f32[128,2,192]{0,2,1:T(8,128)S(1)} %add.109), channel_id=1, source_target_pairs={{480,0},{0,32},{32,64},{64,96},{96,128},{128,160},{160,192},{192,2... | collective-permute-start | bytes 589832 | tf_op jit(solution)/shard_map/while/body/eval_jaxpr/ppermute | solution.py:22
  (27 other events, 308.0 us)
Sparse Core Ops, SparseCore 0:
  11.3 78.6 all-gather.1
where the time goes:
time: 499 us; the launch traced here: 495 us
  starting transfers between devices  239 us (48%)
  waiting for transfers between devices  123 us (25%)
  local copies, waits for them, and re-layouts  53.8 us (11%)
  other arithmetic  51.3 us (10%)
  between operations  14.3 us (3%)
  matrix products  11.1 us (2%)
    ppermute x32, starting transfers between devices, passed_along(): return lax.ppermute(block, axis, route)  124 us
    ppermute x32, starting transfers between devices, shifted(): return lax.ppermute(block, axis, route)  91.8 us
    ppermute x32, waiting for transfers between devices, passed_along(): return lax.ppermute(block, axis, route)  70.4 us
    all_to_all x1, waiting for transfers between devices, local(): lax.all_to_all(sent, 'ep', split_axis=0, concat_axis=3, tiled=True)  52.3 us
    unnamed x2, other arithmetic  39.8 us
    while x32, local copies, waits for them, and re-layouts  20.4 us
    all_to_all x1, starting transfers between devices, local(): lax.all_to_all(sent, 'ep', split_axis=0, concat_axis=3, tiled=True)  16.3 us
    unnamed x30, local copies, waits for them, and re-layouts  14.6 us
  transfers between devices with their start and end apart: 67, of which 17 were waited for; matrix products, arithmetic and copies ran while one was open for 22% of the time, Pallas kernels for 0%

commit v1 on v0

v1 whole, which is shorter than its diff:
```python
import jax
import jax.numpy as jnp
from jax import lax
from jax.experimental import pallas as pl
from jax.experimental.pallas import tpu as pltpu
from jax.sharding import PartitionSpec as P

QK = 192
DH = 128
CAP = 64
SCALE = QK ** (-0.5)
MESH = pl.DeviceIdType.MESH
F32 = jnp.float32
BF16 = jnp.bfloat16


def dot_nn(a, b):
    return lax.dot_general(a, b, (((1,), (0,)), ((), ())), preferred_element_type=F32)


def dot_nt(a, b):
    return lax.dot_general(a, b, (((1,), (1,)), ((), ())), preferred_element_type=F32)


def dot_tn(a, b):
    return lax.dot_general(a, b, (((0,), (0,)), ((), ())), preferred_element_type=F32)


def kernel(
    q_ref,
    k_ref,
    v_ref,
    do_ref,
    o_ref,
    ln_ref,
    lg_ref,
    gp_ref,
    id_ref,
    hid_ref,
    qg_ref,
    kg_ref,
    vg_ref,
    dg_ref,
    own_a,
    own_b,
    own_l,
    sw_a,
    sw_b,
    sw_l,
    ra,
    rb,
    rl,
    acc_a,
    acc_v,
    fo_a,
    fo_b,
    fi_a,
    fi_b,
    ring,
    send,
    cols,
    hid,
    sw_s,
    sw_r,
    at_s,
    at_r,
    fo_s,
    fo_r,
    rg_s,
    rg_r,
    cl_s,
    cl_r,
    loc_s,
    ho_s,
    ha_s,
    hb_s,
    hd_s,
    h_r,
):
    c = lax.axis_index("cp")
    e = lax.axis_index("ep")
    core = c % 2
    chip = c // 2
    z = e % 16
    xl = e // 16
    sib = c + 1 - 2 * core
    xpart = c + 2 - 4 * (chip % 2)

    def at_cp(other):
        return (other, e)

    def remote(src, dst, s_sem, r_sem, target):
        return pltpu.make_async_remote_copy(
            src_ref=src,
            dst_ref=dst,
            send_sem=s_sem,
            recv_sem=r_sem,
            device_id=target,
            device_id_type=MESH,
        )

    barrier = pltpu.get_barrier_semaphore()
    zup = xl * 16 + (z + 1) % 16
    zdown = xl * 16 + (z + 15) % 16
    cross = e + 16 - 32 * xl

    def greet_cp(n, carry):
        pl.semaphore_signal(barrier, inc=1, device_id=at_cp((c + n) % 16), device_id_type=MESH)
        return carry

    lax.fori_loop(1, 16, greet_cp, 0)
    pl.semaphore_signal(barrier, inc=1, device_id=(c, zup), device_id_type=MESH)
    pl.semaphore_signal(barrier, inc=1, device_id=(c, zdown), device_id_type=MESH)

    @pl.when(c // 8 != xl)
    def _():
        def greet_cross(n, carry):
            pl.semaphore_signal(barrier, inc=1, device_id=(n, cross), device_id_type=MESH)
            return carry

        lax.fori_loop(0, 16, greet_cross, 0)

    first = core == 0
    mine = pl.ds(pl.multiple_of(core * 128, 128), 128)

    def halves(ref, width):
        return ref[:, 0:width], ref[:, width : 2 * width]

    prod = do_ref[...].astype(F32) * o_ref[...].astype(F32)
    d0 = jnp.sum(prod[:, 0:DH], axis=1, keepdims=True)
    d1 = jnp.sum(prod[:, DH : 2 * DH], axis=1, keepdims=True)
    lane = lax.broadcasted_iota(jnp.int32, (128, 128), 1)
    both = jnp.where(lane == 0, d0, jnp.where(lane == 1, d1, 0.0))
    rows_d = both.T[0:8, :]
    rows_n = ln_ref[...]
    sub = lax.broadcasted_iota(jnp.int32, (8, 128), 0)
    l0 = jnp.where(sub == 0, rows_n[0:1, :], rows_d[0:1, :])
    l1 = jnp.where(sub == 0, rows_n[1:2, :], rows_d[1:2, :])
    own_l[core] = jnp.where(first, l0, l1)
    sw_l[...] = jnp.where(first, l1, l0)
    for n, ref in enumerate((q_ref, k_ref)):
        h0, h1 = halves(ref, QK)
        own_a[n, mine, :] = jnp.where(first, h0, h1)
        sw_a[n] = jnp.where(first, h1, h0)
    for n, ref in enumerate((do_ref, v_ref)):
        h0, h1 = halves(ref, DH)
        own_b[n, mine, :] = jnp.where(first, h0, h1)
        sw_b[n] = jnp.where(first, h1, h0)
    ring[z] = lg_ref[...]
    hid[c] = hid_ref[0]

    pl.semaphore_wait(barrier, 25)

    swaps = [
        remote(sw_a, own_a.at[:, mine, :], sw_s.at[0], sw_r.at[0], at_cp(sib)),
        remote(sw_b, own_b.at[:, mine, :], sw_s.at[1], sw_r.at[1], at_cp(sib)),
        remote(sw_l, own_l.at[core], sw_s.at[2], sw_r.at[2], at_cp(sib)),
    ]
    for copy in swaps:
        copy.start()

    def ring_copy(up, s):
        block = (z + 16 - s) % 16 if up else (z + s) % 16
        n = 0 if up else 1
        if isinstance(s, int) and s == 7:
            ref = ring.at[block, pl.ds(64 * n, 64), :]
        else:
            ref = ring.at[block]
        return remote(ref, ref, rg_s.at[n, s], rg_r.at[n, s], (c, zup if up else zdown))

    ring_copy(True, 0).start()
    ring_copy(False, 0).start()

    half_a, half_b = pl.ds(0, 32), pl.ds(32, 32)

    def ypeer(n):
        return (c + 4 * n) % 16

    def piece(owner, half):
        return hid.at[owner, half, :]

    def own_piece(n, target, half, col):
        return remote(
            piece(c, half), piece(c, half), ho_s.at[col, n], h_r.at[col, c], at_cp(target)
        )

    own_sends = [own_piece(0, xpart, half_a, 0)]
    own_sends += [own_piece(n, ypeer(n), half_b, 1) for n in (1, 3, 2)]
    for copy in own_sends:
        copy.start()
    for copy in swaps:
        copy.wait_recv()

    def att_copies(n):
        other = (c + 2 * n) % 16
        pick = jnp.where(other // 2 > chip, 1, 0)
        return (
            remote(own_a.at[pick], ra.at[chip], at_s.at[0, n], at_r.at[0, chip], at_cp(other)),
            remote(own_b.at[pick], rb.at[chip], at_s.at[1, n], at_r.at[1, chip], at_cp(other)),
            remote(own_l, rl.at[chip], at_s.at[2, n], at_r.at[2, chip], at_cp(other)),
        )

    def att_start(n, carry):
        for copy in att_copies(n):
            copy.start()
        return carry

    lax.fori_loop(1, 8, att_start, 0)
    later = [own_piece(n, ypeer(n), half_a, 0) for n in (1, 3, 2)]
    later.append(own_piece(0, xpart, half_b, 1))
    for copy in later:
        copy.start()
    own_sends += later
    whole = remote(hid.at[c], hid.at[c], ho_s.at[2, 0], h_r.at[2, c], at_cp(sib))
    whole.start()

    own_rows = own_l[...]
    norm_row = jnp.concatenate([own_rows[0, 0:1, :], own_rows[1, 0:1, :]], axis=1)
    delta_row = jnp.concatenate([own_rows[0, 1:2, :], own_rows[1, 1:2, :]], axis=1)
    col0 = jnp.concatenate([own_rows[0], jnp.zeros((120, 128), F32)], axis=0).T
    col1 = jnp.concatenate([own_rows[1], jnp.zeros((120, 128), F32)], axis=0).T
    norm_col = jnp.concatenate([col0[:, 0:1], col1[:, 0:1]], axis=0)
    delta_col = jnp.concatenate([col0[:, 1:2], col1[:, 1:2]], axis=0)

    def block(x, y, a, b, norm, delta, mask):
        probs = jnp.exp(SCALE * dot_nt(x, a) - norm)
        if mask is not None:
            probs = jnp.where(mask, probs, 0.0)
        ds = (probs * (dot_nt(y, b) - delta)).astype(BF16)
        return dot_nn(ds, a), dot_nn(probs.astype(BF16), b)

    r_iota = lax.broadcasted_iota(jnp.int32, (256, 256), 0)
    c_iota = lax.broadcasted_iota(jnp.int32, (256, 256), 1)
    q_part, _ = block(
        own_a[0], own_b[0], own_a[1], own_b[1], norm_col, delta_col, r_iota >= c_iota
    )
    k_part, v_part = block(
        own_a[1], own_b[1], own_a[0], own_b[0], norm_row, delta_row, c_iota >= r_iota
    )
    acc_a[0] = q_part
    acc_a[1] = k_part
    acc_v[0] = jnp.zeros((256, DH), F32)
    acc_v[1] = v_part

    def att_step(n):
        other = (chip + 8 - n) % 8
        for copy in (
            remote(own_a.at[0], ra.at[other], at_s.at[0, n], at_r.at[0, other], at_cp(sib)),
            remote(own_b.at[0], rb.at[other], at_s.at[1, n], at_r.at[1, other], at_cp(sib)),
            remote(own_l, rl.at[other], at_s.at[2, n], at_r.at[2, other], at_cp(sib)),
        ):
            copy.wait_recv()
        side = jnp.where(other > chip, 1, 0)
        rows = rl[other]
        far_norm = jnp.concatenate([rows[0, 0:1, :], rows[1, 0:1, :]], axis=1)
        far_delta = jnp.concatenate([rows[0, 1:2, :], rows[1, 1:2, :]], axis=1)
        is_far = other > chip
        norm = jnp.where(is_far, far_norm, norm_col)
        delta = jnp.where(is_far, far_delta, delta_col)
        part_a, part_v = block(
            own_a[side], own_b[side], ra[other], rb[other], norm, delta, None
        )
        acc_a[side] += part_a
        acc_v[side] += part_v

    def turn(n, carry):
        ring_copy(True, n - 1).wait_recv()
        ring_copy(True, n).start()
        ring_copy(False, n - 1).wait_recv()
        ring_copy(False, n).start()
        att_step(n)
        return carry

    def turn_ring(up, s):
        ring_copy(up, s).start()

    def arrived(owner, half, col):
        remote(piece(owner, half), piece(owner, half), hd_s.at[col, 0], h_r.at[col, owner], at_cp(sib)).wait_recv()

    def to_sibling(owner, half, col, n):
        return remote(
            piece(owner, half), piece(owner, half), hd_s.at[col, n], h_r.at[col, owner], at_cp(sib)
        )

    sib_sends = []
    fwd_sends = []
    lax.fori_loop(1, 2, turn, 0)
    arrived(xpart, half_a, 0)
    for n in (1, 3, 2):
        copy = remote(
            piece(xpart, half_a), piece(xpart, half_a), ha_s.at[n], h_r.at[0, xpart], at_cp(ypeer(n))
        )
        copy.start()
        fwd_sends.append(copy)
    sib_sends.append(to_sibling(xpart, half_a, 0, 0))
    sib_sends[-1].start()
    lax.fori_loop(2, 3, turn, 0)
    for n in (1, 3, 2):
        arrived(ypeer(n), half_b, 1)
        copy = remote(
            piece(ypeer(n), half_b), piece(ypeer(n), half_b), hb_s.at[n], h_r.at[1, ypeer(n)], at_cp(xpart)
        )
        copy.start()
        fwd_sends.append(copy)
        sib_sends.append(to_sibling(ypeer(n), half_b, 1, n))
        sib_sends[-1].start()
    lax.fori_loop(3, 7, turn, 0)
    ring_copy(True, 6).wait_recv()
    ring_copy(False, 6).wait_recv()
    ring_copy(True, 7).start()
    ring_copy(False, 7).start()
    att_step(7)

    ids = id_ref[...]
    gates = gp_ref[...]
    tri = (lax.broadcasted_iota(jnp.int32, (128, 128), 0) > lane).astype(BF16)
    table = jnp.zeros((128, 128), F32)
    weight = jnp.zeros((128, 128), F32)
    for n in range(2):
        hit = ids == 16 * n + z
        named = jnp.sum(jnp.where(hit, 1.0, 0.0), axis=1, keepdims=True)
        gate = jnp.sum(jnp.where(hit, gates, 0.0), axis=1, keepdims=True)
        before = dot_nn(tri, jnp.broadcast_to(named, (128, 128)).astype(BF16))
        place = before + (CAP * n)
        inside = (place == lane.astype(F32)) & (named > 0.5)
        table = jnp.where(inside, 1.0, table)
        weight = jnp.where(inside, gate, weight)
    onehot = table.T.astype(BF16)
    slot_gate = jnp.sum(weight.T, axis=1, keepdims=True)

    ring_copy(True, 7).wait_recv()
    ring_copy(False, 7).wait_recv()

    def col_target(k):
        return xl * 8 + k

    def col_copy(k, n):
        return remote(
            send.at[k, n], cols.at[c], cl_s.at[k, n], cl_r.at[c], (col_target(k), n * 16 + z)
        )

    def col_local(k, n):
        return pltpu.make_async_copy(send.at[k, n], cols.at[c], loc_s)

    def dispatch(k, carry):
        rows = jnp.concatenate([ring[2 * k], ring[2 * k + 1]], axis=1)
        out = (slot_gate * dot_nn(onehot, rows)).astype(BF16)
        for n in range(2):
            send[k, n] = out[n * CAP : (n + 1) * CAP, :]
            here = (col_target(k) == c) & (n == xl)

            @pl.when(here)
            def _():
                col_local(k, n).start()

            @pl.when(jnp.logical_not(here))
            def _():
                col_copy(k, n).start()

        return carry

    lax.fori_loop(0, 8, dispatch, 0)

    theirs = pl.ds(pl.multiple_of((1 - core) * 128, 128), 128)
    for n in range(2):
        fo_a[n] = (SCALE * acc_a[n, theirs, :]).astype(BF16)
    fo_b[...] = acc_v[1, theirs, :].astype(BF16)
    backs = [
        remote(fo_a, fi_a, fo_s.at[0], fo_r.at[0], at_cp(sib)),
        remote(fo_b, fi_b, fo_s.at[1], fo_r.at[1], at_cp(sib)),
    ]
    for copy in backs:
        copy.start()

    for n in (1, 3, 2):
        arrived(ypeer(n), half_a, 0)
        sib_sends.append(to_sibling(ypeer(n), half_a, 0, n))
        sib_sends[-1].start()
    arrived(xpart, half_b, 1)
    sib_sends.append(to_sibling(xpart, half_b, 1, 0))
    sib_sends[-1].start()
    for n in (1, 3, 2):
        far = (xpart + 4 * n) % 16
        arrived(far, half_a, 0)
        sib_sends.append(to_sibling(far, half_a, 0, 4 + n))
        sib_sends[-1].start()
        arrived(far, half_b, 1)
        sib_sends.append(to_sibling(far, half_b, 1, 4 + n))
        sib_sends[-1].start()

    for copy in backs:
        copy.wait()
    for n, ref in enumerate((qg_ref, kg_ref)):
        kept = (SCALE * acc_a[n, mine, :]).astype(BF16)
        got = fi_a[n]
        ref[:, 0:QK] = jnp.where(first, kept, got)
        ref[:, QK : 2 * QK] = jnp.where(first, got, kept)
    kept = acc_v[1, mine, :].astype(BF16)
    got = fi_b[...]
    vg_ref[:, 0:DH] = jnp.where(first, kept, got)
    vg_ref[:, DH : 2 * DH] = jnp.where(first, got, kept)

    remote(hid.at[sib], hid.at[sib], ho_s.at[2, 0], h_r.at[2, sib], at_cp(sib)).wait_recv()

    def from_sibling(n, carry):
        owner = (sib + 2 * n) % 16
        arrived(owner, half_a, 0)
        arrived(owner, half_b, 1)
        return carry

    lax.fori_loop(1, 8, from_sibling, 0)

    def col_wait(n, carry):
        here = (n == c) & (c // 8 == xl)

        @pl.when(here)
        def _():
            pltpu.make_async_copy(send.at[0, 0], cols.at[n], loc_s).wait()

        @pl.when(jnp.logical_not(here))
        def _():
            remote(send.at[0, 0], cols.at[n], cl_s.at[0, 0], cl_r.at[n], at_cp(sib)).wait_recv()

        return carry

    lax.fori_loop(0, 16, col_wait, 0)

    right = cols[...].reshape(16 * CAP, 448)

    def product(n, carry):
        tile = pl.ds(pl.multiple_of(n * 256, 256), 256)
        left = hid[:, :, tile].reshape(16 * CAP, 256)
        dg_ref[0, tile, :] = dot_tn(left, right).astype(BF16)
        return carry

    lax.fori_loop(0, 8, product, 0)

    for copy in swaps + own_sends + fwd_sends + sib_sends + [whole]:
        copy.wait_send()

    def att_sent(n, carry):
        for copy in att_copies(n):
            copy.wait_send()
        return carry

    lax.fori_loop(1, 8, att_sent, 0)

    def ring_sent(s, carry):
        ring_copy(True, s).wait_send()
        ring_copy(False, s).wait_send()
        return carry

    lax.fori_loop(0, 7, ring_sent, 0)
    ring_copy(True, 7).wait_send()
    ring_copy(False, 7).wait_send()

    def cols_sent(k, carry):
        for n in range(2):

            @pl.when(jnp.logical_not((col_target(k) == c) & (n == xl)))
            def _():
                col_copy(k, n).wait_send()

        return carry

    lax.fori_loop(0, 8, cols_sent, 0)


def local(*args):
    vmem = pl.BlockSpec(memory_space=pltpu.VMEM)
    dma = pltpu.SemaphoreType.DMA
    return pl.pallas_call(
        kernel,
        out_shape=(
            jax.ShapeDtypeStruct((128, 2 * QK), BF16),
            jax.ShapeDtypeStruct((128, 2 * QK), BF16),
            jax.ShapeDtypeStruct((128, 2 * DH), BF16),
            jax.ShapeDtypeStruct((1, 2048, 448), BF16),
        ),
        in_specs=[vmem] * 10,
        out_specs=(vmem,) * 4,
        scratch_shapes=[
            pltpu.VMEM((2, 256, QK), BF16),
            pltpu.VMEM((2, 256, DH), BF16),
            pltpu.VMEM((2, 8, 128), F32),
            pltpu.VMEM((2, 128, QK), BF16),
            pltpu.VMEM((2, 128, DH), BF16),
            pltpu.VMEM((8, 128), F32),
            pltpu.VMEM((8, 256, QK), BF16),
            pltpu.VMEM((8, 256, DH), BF16),
            pltpu.VMEM((8, 2, 8, 128), F32),
            pltpu.VMEM((2, 256, QK), F32),
            pltpu.VMEM((2, 256, DH), F32),
            pltpu.VMEM((2, 128, QK), BF16),
            pltpu.VMEM((128, DH), BF16),
            pltpu.VMEM((2, 128, QK), BF16),
            pltpu.VMEM((128, DH), BF16),
            pltpu.VMEM((16, 128, 224), BF16),
            pltpu.VMEM((8, 2, CAP, 448), BF16),
            pltpu.VMEM((16, CAP, 448), BF16),
            pltpu.VMEM((16, CAP, 2048), BF16),
            dma((3,)),
            dma((3,)),
            dma((3, 8)),
            dma((3, 8)),
            dma((2,)),
            dma((2,)),
            dma((2, 8)),
            dma((2, 8)),
            dma((8, 2)),
            dma((16,)),
            dma,
            dma((3, 4)),
            dma((4,)),
            dma((4,)),
            dma((2, 8)),
            dma((3, 16)),
        ],
        compiler_params=pltpu.CompilerParams(
            collective_id=0, has_side_effects=True, vmem_limit_bytes=48 * 2**20
        ),
    )(*args)


def solution(mesh):
    return jax.shard_map(
        local,
        mesh=mesh,
        in_specs=(
            P("cp", "ep"),
            P("cp", "ep"),
            P("cp", "ep"),
            P("cp", "ep"),
            P("cp", "ep"),
            P("ep", "cp"),
            P("cp", "ep"),
            P("cp", None),
            P("cp", None),
            P("ep", "cp", None),
        ),
        out_specs=(P("cp", "ep"), P("cp", "ep"), P("cp", "ep"), P("ep", None, "cp")),
        check_vma=False,
    )
```

time: 499 us -> 86.9 us (0.17)
  the two profiles are of different devices: /device:TPU:32 before, /device:TPU:9 now
where the time goes in v1:
time: 86.9 us; the launch traced here: 86.5 us
  Pallas kernels  73.2 us (84%)
  local copies, waits for them, and re-layouts  12.6 us (14%)
    pallas_call x1, Pallas kernels, local(): pl.pallas_call(kernel, out_shape=(jax.ShapeDtypeStruct((128, 2 * QK), BF1...  73.2 us
    unnamed x20, local copies, waits for them, and re-layouts  10.3 us
    pallas_call x1, local copies, waits for them, and re-layouts, local(): pl.pallas_call(kernel, out_shape=(jax.ShapeDtypeStruct((128, 2 * QK), BF1...  2.29 us

profile of v1, /device:TPU:9, one launch (start us, length us, event | category | flops | bytes accessed | tf_op | source)
XLA Modules:
  0.0 86.5 jit_solution(3527064494954777441)
XLA Ops:
  0.6 0.9 %copy.14.lg_ref = bf16[128,224]{1,0:T(8,128)(2,1)S(1)} copy(bf16[128,224]{0,1:T(8,128)(2,1)} %param.16) | data formatting | bytes 114688 | tf_op args[6]
  1.6 0.8 copy.15.gp_ref
  2.3 0.8 copy.16.id_ref
  3.1 0.0 copy-start
  3.1 0.9 %copy-done = bf16[1,64,2048]{2,1,0:T(8,128)(2,1)S(1)} copy-done((bf16[1,64,2048]{2,1,0:T(8,128)(2,1)S(1)}, bf16[1,64,2048]{2,1,0:T(8,128)(2,1)}, u32[]{:S(2)}) %copy-start) | copy-done | bytes 262168
  4.1 0.0 copy-start.1
  4.1 0.9 %copy-done.1 = bf16[128,384]{1,0:T(8,128)(2,1)S(1)} copy-done((bf16[128,384]{1,0:T(8,128)(2,1)S(1)}, bf16[128,384]{1,0:T(8,128)(2,1)}, u32[]{:S(2)}) %copy-start.1) | copy-done | bytes 98328
  5.0 0.0 copy-start.2
  5.0 0.9 %copy-done.2 = bf16[128,384]{1,0:T(8,128)(2,1)S(1)} copy-done((bf16[128,384]{1,0:T(8,128)(2,1)S(1)}, bf16[128,384]{1,0:T(8,128)(2,1)}, u32[]{:S(2)}) %copy-start.2) | copy-done | bytes 98328
  5.9 0.0 copy-start.3
  5.9 0.8 copy-done.3
  6.7 0.0 copy-start.4
  6.7 0.8 copy-done.4
  7.5 0.0 copy-start.5
  7.5 0.8 copy-done.5
  8.4 0.0 copy-start.6
  8.4 0.7 copy-done.6
  9.1 73.2 %shard_map.129 = (bf16[128,384]{1,0:T(8,128)(2,1)S(1)}, bf16[128,384]{1,0:T(8,128)(2,1)S(1)}, bf16[128,256]{1,0:T(8,128)(2,1)S(1)}, bf16[1,2048,448]{2,1,0:T(8,128)(2,1)S(1)}) custom-call(bf16[128,384]{1,0:T(8,128)(2,1)S(1)} %copy-done.1, bf16[128,384]{1,0:T(8,128)(2,1)S(1)} %copy-done.2, bf16[128,256]{1,0:T(8,128)(2,1)S(1)} %copy-done.3, ...), custom_call_target="tpu_custom_call" | custom-call | tf_op jit(solution)/shard_map/pallas_call | solution.py:472
  82.3 2.3 %copy.17 = bf16[1,2048,448]{1,2,0:T(8,128)(2,1)} copy(bf16[1,2048,448]{2,1,0:T(8,128)(2,1)S(1)} %get-tuple-element.7) | data formatting | bytes 3670016 | tf_op jit(solution)/shard_map/pallas_call | solution.py:472
  84.5 0.6 copy.21
  85.2 0.6 copy.22
  85.8 0.6 copy.23
Async XLA Ops:
  3.1 0.9 %copy-start = (bf16[1,64,2048]{2,1,0:T(8,128)(2,1)S(1)}, bf16[1,64,2048]{2,1,0:T(8,128)(2,1)}, u32[]{:S(2)}) copy-start(bf16[1,64,2048]{2,1,0:T(8,128)(2,1)} %hid_ref.1) | copy-start | bytes 786436
  4.1 0.9 %copy-start.1 = (bf16[128,384]{1,0:T(8,128)(2,1)S(1)}, bf16[128,384]{1,0:T(8,128)(2,1)}, u32[]{:S(2)}) copy-start(bf16[128,384]{1,0:T(8,128)(2,1)} %q_ref.1) | copy-start | bytes 294916
  5.0 0.9 %copy-start.2 = (bf16[128,384]{1,0:T(8,128)(2,1)S(1)}, bf16[128,384]{1,0:T(8,128)(2,1)}, u32[]{:S(2)}) copy-start(bf16[128,384]{1,0:T(8,128)(2,1)} %k_ref.1) | copy-start | bytes 294916
  5.9 0.8 copy-start.3
  6.7 0.8 copy-start.4
  7.5 0.8 copy-start.5
  8.4 0.7 copy-start.6

commit v2 on v1

v2 whole, which is shorter than its diff:
```python
import jax
import jax.numpy as jnp
from jax import lax
from jax.experimental import pallas as pl
from jax.experimental.pallas import tpu as pltpu
from jax.sharding import PartitionSpec as P

QK = 192
DH = 128
CAP = 64
SHARE = 224
BOTH = QK + DH
SCALE = QK ** (-0.5)
MESH = pl.DeviceIdType.MESH
F32 = jnp.float32
BF16 = jnp.bfloat16


def dot_nn(a, b):
    return lax.dot_general(a, b, (((1,), (0,)), ((), ())), preferred_element_type=F32)


def dot_nt(a, b):
    return lax.dot_general(a, b, (((1,), (1,)), ((), ())), preferred_element_type=F32)


def kernel(
    q_in,
    k_in,
    v_in,
    do_in,
    o_in,
    ln_in,
    lg_in,
    gp_in,
    id_in,
    hid_in,
    qg_ref,
    kg_ref,
    vg_ref,
    dg_ref,
    q_ref,
    k_ref,
    v_ref,
    do_ref,
    o_ref,
    ln_ref,
    gp_ref,
    id_ref,
    own_t,
    own_x,
    own_y,
    own_l,
    sw_t,
    sw_l,
    far_t,
    far_l,
    acc_a,
    acc_v,
    fo_a,
    fo_b,
    fi_a,
    fi_b,
    ring,
    send,
    cols,
    left,
    hid,
    in_s,
    sw_s,
    sw_r,
    at_s,
    at_r,
    fo_s,
    fo_r,
    rg_s,
    rg_r,
    cl_s,
    cl_r,
    ho_s,
    ha_s,
    hb_s,
    hd_s,
    h_r,
):
    c = lax.axis_index("cp")
    e = lax.axis_index("ep")
    core = c % 2
    chip = c // 2
    z = e % 16
    xl = e // 16
    sib = c + 1 - 2 * core
    xpart = c + 2 - 4 * (chip % 2)
    cross = e + 16 - 32 * xl

    def at_cp(other):
        return (other, e)

    def remote(src, dst, s_sem, r_sem, target):
        return pltpu.make_async_remote_copy(
            src_ref=src,
            dst_ref=dst,
            send_sem=s_sem,
            recv_sem=r_sem,
            device_id=target,
            device_id_type=MESH,
        )

    barrier = pltpu.get_barrier_semaphore()

    def greet_cp(n, carry):
        pl.semaphore_signal(barrier, inc=1, device_id=at_cp((c + n) % 16), device_id_type=MESH)
        return carry

    lax.fori_loop(1, 16, greet_cp, 0)
    for far in (1, 2, 4, 8, 12, 14, 15):
        near = xl * 16 + (z + far) % 16
        pl.semaphore_signal(barrier, inc=1, device_id=(c, near), device_id_type=MESH)

    @pl.when(c // 8 != xl)
    def _():
        def greet_cross(n, carry):
            pl.semaphore_signal(barrier, inc=1, device_id=(n, cross), device_id_type=MESH)
            return carry

        lax.fori_loop(0, 16, greet_cross, 0)

    loads = []
    for n, (src, dst) in enumerate(
        (
            (q_in, q_ref),
            (k_in, k_ref),
            (v_in, v_ref),
            (do_in, do_ref),
            (o_in, o_ref),
            (ln_in, ln_ref),
            (lg_in, ring.at[z]),
            (gp_in, gp_ref),
            (id_in, id_ref),
            (hid_in.at[0], hid.at[c]),
        )
    ):
        copy = pltpu.make_async_copy(src, dst, in_s.at[n])
        copy.start()
        loads.append(copy)

    first = core == 0
    mine = pl.ds(pl.multiple_of(core * 128, 128), 128)
    lane = lax.broadcasted_iota(jnp.int32, (128, 128), 1)

    def stage():
        for copy in loads[0:6]:
            copy.wait()
        for side, (wide, narrow) in enumerate(((q_ref, do_ref), (k_ref, v_ref))):
            for ref, size, at in ((wide, QK, 0), (narrow, DH, QK)):
                turned = ref[...].T
                h0, h1 = turned[0:size], turned[size : 2 * size]
                own_t[side, at : at + size, mine] = jnp.where(first, h0, h1)
                sw_t[side, at : at + size, :] = jnp.where(first, h1, h0)
        prod = do_ref[...].astype(F32) * o_ref[...].astype(F32)
        d0 = jnp.sum(prod[:, 0:DH], axis=1, keepdims=True)
        d1 = jnp.sum(prod[:, DH : 2 * DH], axis=1, keepdims=True)
        rows_d = jnp.where(lane == 0, d0, jnp.where(lane == 1, d1, 0.0)).T[0:8, :]
        rows_n = ln_ref[...]
        sub = lax.broadcasted_iota(jnp.int32, (8, 128), 0)
        l0 = jnp.where(sub == 0, rows_n[0:1, :], rows_d[0:1, :])
        l1 = jnp.where(sub == 0, rows_n[1:2, :], rows_d[1:2, :])
        own_l[core] = jnp.where(first, l0, l1)
        sw_l[...] = jnp.where(first, l1, l0)

    def z_copy(group, far, n, first_hand):
        block = (z + 4 * group) % 16
        src = lg_in if first_hand else ring.at[block]
        target = xl * 16 + (z + 16 + far) % 16
        return remote(src, ring.at[block], rg_s.at[group, n], rg_r.at[block], (c, target))

    z_first = [z_copy(0, far, n, True) for n, far in enumerate((4, -4, 8, 1, -1, 2))]
    z_later = [
        [z_copy(group, far, n, False) for n, far in enumerate(fars)]
        for group, fars in ((1, (1, -1, 2, -2)), (3, (-1, 1)), (2, (1, -1, -2)))
    ]

    def z_arrived(block):
        remote(ring.at[block], ring.at[block], rg_s.at[0, 0], rg_r.at[block], at_cp(sib)).wait_recv()

    def z_pass():
        for group, copies in zip((1, 3, 2), z_later):
            z_arrived((z + 4 * group) % 16)
            start(copies)

    swaps = [
        remote(sw_t, own_t.at[:, :, mine], sw_s.at[0], sw_r.at[0], at_cp(sib)),
        remote(sw_l, own_l.at[core], sw_s.at[1], sw_r.at[1], at_cp(sib)),
    ]

    half_a, half_b = pl.ds(0, 32), pl.ds(32, 32)

    def ypeer(n):
        return (c + 4 * n) % 16

    def piece(owner, half):
        return hid.at[owner, half, :]

    def own_piece(n, target, half, col):
        return remote(
            hid_in.at[0, half, :], piece(c, half), ho_s.at[col, n], h_r.at[col, c], at_cp(target)
        )

    own_sends = [
        own_piece(n, target, half, col)
        for n, target, half, col in (
            (0, xpart, half_a, 0),
            (1, ypeer(1), half_a, 0),
            (3, ypeer(3), half_b, 1),
            (0, xpart, half_b, 1),
            (1, ypeer(1), half_b, 1),
            (3, ypeer(3), half_a, 0),
        )
    ]

    def att_copy(origin, source, rows, n, target):
        return (
            remote(source, far_t.at[origin], at_s.at[0, n], at_r.at[0, origin], at_cp(target)),
            remote(rows, far_l.at[origin], at_s.at[1, n], at_r.at[1, origin], at_cp(target)),
        )

    def att_own_copies(n, other):
        pick = jnp.where(other // 2 > chip, 1, 0)
        return att_copy(chip, own_t.at[pick], own_l, n, other)

    def att_passed(n):
        origin = (chip + 8 - 2 * n) % 8
        return att_copy(origin, far_t.at[origin], far_l.at[origin], 3 + n, xpart)

    def att_wait(origin):
        for copy in att_copy(origin, own_t.at[0], own_l, 0, sib):
            copy.wait_recv()

    def att_relay(n):
        att_wait((chip + 8 - 2 * n) % 8)
        start(att_passed(n))

    att_sends = [copy for n in (1, 3, 2) for copy in att_own_copies(n, (c + 4 * n) % 16)]
    att_sends += att_own_copies(0, xpart)
    whole = remote(hid_in.at[0], hid.at[c], ho_s.at[2, 0], h_r.at[2, c], at_cp(sib))

    def start(copies):
        for copy in copies:
            copy.start()

    def col_target(k):
        return xl * 8 + k

    def col_copy(k, n):
        return remote(
            send.at[k, n], cols.at[c], cl_s.at[k, n], cl_r.at[c], (col_target(k), n * 16 + z)
        )

    def dispatch(step, carry):
        k = (z // 2 + step + c // 4 + 2 * (c % 4)) % 8
        r0 = gate_0 * dot_nt(ring[2 * k], table_0)
        r1 = gate_1 * dot_nt(ring[2 * k + 1], table_1)
        for n, rows in enumerate((jnp.where(low, r0, r1), jnp.where(low, r1, r0))):
            send[k, n] = rows.astype(BF16)
            here = (col_target(k) == c) & (n == xl)

            @pl.when(here)
            def _():
                cols[c] = send[k, n]

            @pl.when(jnp.logical_not(here))
            def _():
                col_copy(k, n).start()

        return carry

    def dispatch_all():
        for block in range(1, 16):
            if block % 4:
                z_arrived((z + block) % 16)
        lax.fori_loop(0, 8, dispatch, 0)

    def joined(rows, n):
        return jnp.concatenate([rows[0, n : n + 1, :], rows[1, n : n + 1, :]], axis=1)

    def block(side, at, n, norm, delta, mask):
        a, b = at[n, 0:QK, :], at[n, QK:BOTH, :]
        probs = jnp.exp(SCALE * dot_nn(own_x[side], a) - norm)
        if mask is not None:
            probs = jnp.where(mask, probs, 0.0)
        ds = (probs * (dot_nn(own_y[side], b) - delta)).astype(BF16)
        return dot_nt(ds, a), dot_nt(probs.astype(BF16), b)

    def att_own():
        r_iota = lax.broadcasted_iota(jnp.int32, (256, 256), 0)
        c_iota = lax.broadcasted_iota(jnp.int32, (256, 256), 1)
        q_part, _ = block(0, own_t, 1, norm_col, delta_col, r_iota >= c_iota)
        k_part, v_part = block(1, own_t, 0, norm_row, delta_row, c_iota >= r_iota)
        acc_a[0] = q_part
        acc_a[1] = k_part
        acc_v[0] = jnp.zeros((256, DH), F32)
        acc_v[1] = v_part

    def att_step(other):
        side = jnp.where(other > chip, 1, 0)
        rows = far_l[other]
        is_far = other > chip
        norm = jnp.where(is_far, joined(rows, 0), norm_col)
        delta = jnp.where(is_far, joined(rows, 1), delta_col)
        part_a, part_v = block(side, far_t, other, norm, delta, None)
        acc_a[side] += part_a
        acc_v[side] += part_v

    def att_near(n, carry):
        att_step((chip + 8 - 2 * n) % 8)
        return carry

    def att_far(n, carry):
        other = (xpart // 2 + 8 - 2 * n) % 8
        att_wait(other)
        att_step(other)
        return carry

    sib_sends = []
    fwd_sends = []

    def arrived(owner, half, col):
        remote(
            piece(owner, half), piece(owner, half), hd_s.at[col, 0], h_r.at[col, owner], at_cp(sib)
        ).wait_recv()

    def to_sibling(owner, half, col, n):
        copy = remote(
            piece(owner, half), piece(owner, half), hd_s.at[col, n], h_r.at[col, owner], at_cp(sib)
        )
        copy.start()
        sib_sends.append(copy)

    def forward(owner, half, col, sem, target):
        copy = remote(piece(owner, half), piece(owner, half), sem, h_r.at[col, owner], at_cp(target))
        copy.start()
        fwd_sends.append(copy)

    def far_peer(n):
        return (xpart + 4 * n) % 16

    def relay_x(half, col):
        arrived(xpart, half, col)
        for n in (1, 3):
            forward(xpart, half, col, hb_s.at[2 * col + n // 2], ypeer(n))
        to_sibling(xpart, half, col, 0)

    def relay_y(n, near):
        owner = ypeer(n) if near else far_peer(n)
        half, col = (half_a, 0) if n == 3 else (half_b, 1)
        arrived(owner, half, col)
        forward(owner, half, col, ha_s.at[2 * near + col], ypeer(4 - n))
        to_sibling(owner, half, col, n + 4 * (1 - near))

    def keep_y(n, near, half, col):
        owner = ypeer(n) if near else far_peer(n)
        arrived(owner, half, col)
        to_sibling(owner, half, col, n + 4 * (1 - near))

    pl.semaphore_wait(barrier, 30)
    start(z_first)
    start(own_sends)
    stage()
    start(swaps)

    for copy in loads[6:]:
        copy.wait()
    ids = id_ref[...]
    gates = gp_ref[...]
    before_t = (lax.broadcasted_iota(jnp.int32, (128, 128), 0) < lane).astype(BF16)
    spots = lax.broadcasted_iota(jnp.int32, (CAP, 128), 0).astype(F32)
    tables, weights = [], []
    for n in range(2):
        hit = ids == 16 * n + z
        named = jnp.sum(jnp.where(hit, 1.0, 0.0), axis=0, keepdims=True)
        gate = jnp.sum(jnp.where(hit, gates, 0.0), axis=0, keepdims=True)
        earlier = dot_nn(jnp.broadcast_to(named, (8, 128)).astype(BF16), before_t)[0:1, :]
        inside = (spots == earlier) & (named > 0.5)
        tables.append(jnp.where(inside, 1.0, 0.0))
        weights.append(jnp.where(inside, gate, 0.0))
    table_0 = jnp.concatenate(tables, axis=0).astype(BF16)
    table_1 = jnp.concatenate(tables[::-1], axis=0).astype(BF16)
    gate_0 = jnp.sum(jnp.concatenate(weights, axis=0).T, axis=0, keepdims=True)
    gate_1 = jnp.sum(jnp.concatenate(weights[::-1], axis=0).T, axis=0, keepdims=True)
    low = lax.broadcasted_iota(jnp.int32, (SHARE, 128), 1) < CAP

    for copy in swaps:
        copy.wait_recv()
    start(att_sends)
    start([whole])
    relay_x(half_a, 0)
    relay_x(half_b, 1)
    relay_y(3, 1)
    relay_y(1, 1)
    att_relay(1)
    att_relay(3)
    z_pass()
    att_relay(2)
    relay_y(3, 0)
    relay_y(1, 0)
    for side in range(2):
        own_x[side] = own_t[side, 0:QK, :].T
        own_y[side] = own_t[side, QK:BOTH, :].T

    own_rows = own_l[...]
    norm_row, delta_row = joined(own_rows, 0), joined(own_rows, 1)
    turned_l = [
        jnp.concatenate([own_rows[n], jnp.zeros((120, 128), F32)], axis=0).T for n in range(2)
    ]
    norm_col = jnp.concatenate([turned_l[0][:, 0:1], turned_l[1][:, 0:1]], axis=0)
    delta_col = jnp.concatenate([turned_l[0][:, 1:2], turned_l[1][:, 1:2]], axis=0)
    att_own()
    lax.fori_loop(1, 4, att_near, 0)
    dispatch_all()
    lax.fori_loop(0, 4, att_far, 0)
    theirs = pl.ds(pl.multiple_of((1 - core) * 128, 128), 128)
    for n in range(2):
        fo_a[n] = (SCALE * acc_a[n, theirs, :]).astype(BF16)
    fo_b[...] = acc_v[1, theirs, :].astype(BF16)
    backs = [
        remote(fo_a, fi_a, fo_s.at[0], fo_r.at[0], at_cp(sib)),
        remote(fo_b, fi_b, fo_s.at[1], fo_r.at[1], at_cp(sib)),
    ]
    for copy in backs:
        copy.start()
    for near in (1, 0):
        keep_y(1, near, half_a, 0)
        keep_y(3, near, half_b, 1)
        keep_y(2, near, half_a, 0)
        keep_y(2, near, half_b, 1)

    for copy in backs:
        copy.wait()
    for n, ref in enumerate((qg_ref, kg_ref)):
        kept = (SCALE * acc_a[n, mine, :]).astype(BF16)
        got = fi_a[n]
        ref[:, 0:QK] = jnp.where(first, kept, got)
        ref[:, QK : 2 * QK] = jnp.where(first, got, kept)
    kept = acc_v[1, mine, :].astype(BF16)
    got = fi_b[...]
    vg_ref[:, 0:DH] = jnp.where(first, kept, got)
    vg_ref[:, DH : 2 * DH] = jnp.where(first, got, kept)

    remote(hid.at[sib], hid.at[sib], ho_s.at[2, 0], h_r.at[2, sib], at_cp(sib)).wait_recv()

    def from_sibling(n, carry):
        owner = (sib + 2 * n) % 16
        arrived(owner, half_a, 0)
        arrived(owner, half_b, 1)
        return carry

    lax.fori_loop(1, 8, from_sibling, 0)

    def col_wait(n, carry):
        @pl.when(jnp.logical_not((n == c) & (c // 8 == xl)))
        def _():
            remote(send.at[0, 0], cols.at[n], cl_s.at[0, 0], cl_r.at[n], at_cp(sib)).wait_recv()

        return carry

    lax.fori_loop(0, 16, col_wait, 0)

    for m in range(8):
        p0, p1 = cols[2 * m], cols[2 * m + 1]
        t0 = jnp.concatenate([p0[:, 0:CAP], p1[:, 0:CAP]], axis=1)
        t1 = jnp.concatenate([p0[:, CAP : 2 * CAP], p1[:, CAP : 2 * CAP]], axis=1)
        left[0:SHARE, 128 * m : 128 * m + 128] = jnp.where(xl == 0, t0, t1)
        left[SHARE : 2 * SHARE, 128 * m : 128 * m + 128] = jnp.where(xl == 0, t1, t0)

    def product(n, carry):
        tile = pl.ds(pl.multiple_of(n * 256, 256), 256)
        right = hid[:, :, tile].reshape(16 * CAP, 256)
        dg_ref[0, :, tile] = dot_nn(left[...], right).astype(BF16)
        return carry

    lax.fori_loop(0, 8, product, 0)

    for copy in swaps + own_sends + fwd_sends + sib_sends + [whole] + att_sends + z_first + sum(z_later, []):
        copy.wait_send()

    for n in (1, 2, 3):
        for copy in att_passed(n):
            copy.wait_send()

    def cols_sent(k, carry):
        for n in range(2):

            @pl.when(jnp.logical_not((col_target(k) == c) & (n == xl)))
            def _():
                col_copy(k, n).wait_send()

        return carry

    lax.fori_loop(0, 8, cols_sent, 0)


def put_out(*refs):
    ins, outs, sems = refs[0:4], refs[4:8], refs[8]
    copies = [pltpu.make_async_copy(a, b, sems.at[n]) for n, (a, b) in enumerate(zip(ins, outs))]
    for copy in copies:
        copy.start()
    for copy in copies:
        copy.wait()


def local(q, k, v, do, o, ln, lg, gp, ids, hidden):
    vmem = pl.BlockSpec(memory_space=pltpu.VMEM)
    hbm = pl.BlockSpec(memory_space=pltpu.HBM)
    dma = pltpu.SemaphoreType.DMA
    shapes = (
        jax.ShapeDtypeStruct((128, 2 * QK), BF16),
        jax.ShapeDtypeStruct((128, 2 * QK), BF16),
        jax.ShapeDtypeStruct((128, 2 * DH), BF16),
        jax.ShapeDtypeStruct((1, 2 * SHARE, 2048), BF16),
    )
    results = pl.pallas_call(
        kernel,
        out_shape=shapes,
        in_specs=[hbm] * 10,
        out_specs=(vmem,) * 4,
        scratch_shapes=[
            pltpu.VMEM((128, 2 * QK), BF16),
            pltpu.VMEM((128, 2 * QK), BF16),
            pltpu.VMEM((128, 2 * DH), BF16),
            pltpu.VMEM((128, 2 * DH), BF16),
            pltpu.VMEM((128, 2 * DH), BF16),
            pltpu.VMEM((2, 128), F32),
            pltpu.VMEM((8, 128), F32),
            pltpu.VMEM((8, 128), jnp.int32),
            pltpu.VMEM((2, BOTH, 256), BF16),
            pltpu.VMEM((2, 256, QK), BF16),
            pltpu.VMEM((2, 256, DH), BF16),
            pltpu.VMEM((2, 8, 128), F32),
            pltpu.VMEM((2, BOTH, 128), BF16),
            pltpu.VMEM((8, 128), F32),
            pltpu.VMEM((8, BOTH, 256), BF16),
            pltpu.VMEM((8, 2, 8, 128), F32),
            pltpu.VMEM((2, 256, QK), F32),
            pltpu.VMEM((2, 256, DH), F32),
            pltpu.VMEM((2, 128, QK), BF16),
            pltpu.VMEM((128, DH), BF16),
            pltpu.VMEM((2, 128, QK), BF16),
            pltpu.VMEM((128, DH), BF16),
            pltpu.VMEM((16, SHARE, 128), BF16),
            pltpu.VMEM((8, 2, SHARE, 128), BF16),
            pltpu.VMEM((16, SHARE, 128), BF16),
            pltpu.VMEM((2 * SHARE, 16 * CAP), BF16),
            pltpu.VMEM((16, CAP, 2048), BF16),
            dma((10,)),
            dma((2,)),
            dma((2,)),
            dma((2, 8)),
            dma((2, 8)),
            dma((2,)),
            dma((2,)),
            dma((4, 6)),
            dma((16,)),
            dma((8, 2)),
            dma((16,)),
            dma((3, 4)),
            dma((4,)),
            dma((4,)),
            dma((2, 8)),
            dma((3, 16)),
        ],
        compiler_params=pltpu.CompilerParams(
            collective_id=0, has_side_effects=True, vmem_limit_bytes=60 * 2**20
        ),
    )(q, k, v, do, o, ln, lg.T, gp.T, ids.T, hidden)
    q_grad, k_grad, v_grad, down = pl.pallas_call(
        put_out,
        out_shape=shapes,
        in_specs=[vmem] * 4,
        out_specs=(hbm,) * 4,
        scratch_shapes=[dma((4,))],
    )(*results)
    return q_grad, k_grad, v_grad, jnp.swapaxes(down, 1, 2)


def solution(mesh):
    return jax.shard_map(
        local,
        mesh=mesh,
        in_specs=(
            P("cp", "ep"),
            P("cp", "ep"),
            P("cp", "ep"),
            P("cp", "ep"),
            P("cp", "ep"),
            P("ep", "cp"),
            P("cp", "ep"),
            P("cp", None),
            P("cp", None),
            P("ep", "cp", None),
        ),
        out_specs=(P("cp", "ep"), P("cp", "ep"), P("cp", "ep"), P("ep", None, "cp")),
        check_vma=False,
    )
```

time: 86.9 us -> 65.4 us (0.75)
  the two profiles are of different devices: /device:TPU:9 before, /device:TPU:7 now
where the time goes in v2:
time: 65.4 us; the launch traced here: 65.2 us
  Pallas kernels  64.6 us (99%)
    pallas_call x1, Pallas kernels, local(): pl.pallas_call(kernel, out_shape=shapes, in_specs=[hbm] * 10, out_specs=(...  61.6 us
    pallas_call x1, Pallas kernels, local(): pl.pallas_call(put_out, out_shape=shapes, in_specs=[vmem] * 4, out_specs=...  3.01 us

profile of v2, /device:TPU:7, one launch (start us, length us, event | category | flops | bytes accessed | tf_op | source)
XLA Modules:
  0.0 65.2 jit_solution(1971261807926913038)
XLA Ops:
  0.6 61.6 %shard_map.129 = (bf16[128,384]{1,0:T(8,128)(2,1)}, bf16[128,384]{1,0:T(8,128)(2,1)}, bf16[128,256]{1,0:T(8,128)(2,1)}, bf16[1,448,2048]{2,1,0:T(8,128)(2,1)}) custom-call(bf16[128,384]{1,0:T(8,128)(2,1)} %q_in.1, bf16[128,384]{1,0:T(8,128)(2,1)} %k_in.1, bf16[128,256]{1,0:T(8,128)(2,1)} %v_in.1, bf16[128,256]{1,0:T(8,128)(2,1)} %do_in.1, ...), custom_call_target="tpu_custom_call" | custom-call | tf_op jit(solution)/shard_map/pallas_call | solution.py:521
  62.2 3.0 %shard_map.130 = (bf16[128,384]{1,0:T(8,128)(2,1)}, bf16[128,384]{1,0:T(8,128)(2,1)}, bf16[128,256]{1,0:T(8,128)(2,1)}, bf16[1,448,2048]{2,1,0:T(8,128)(2,1)}) custom-call(bf16[128,384]{1,0:T(8,128)(2,1)} %get-tuple-element.12.refs_0_, bf16[128,384]{1,0:T(8,128)(2,1)} %get-tuple-element.13.refs_1_, bf16[128,256]{1,0:T(8,128)(2,1)} %get-tuple-element.14.refs_2_, ...), custom_call_target="tpu_custom_call" | custom-call | tf_op jit(solution)/shard_map/pallas_call | solution.py:575

commit v3 on v2

--- a/solution.py
+++ b/solution.py
@@ -113,7 +113,7 @@
         return carry
 
     lax.fori_loop(1, 16, greet_cp, 0)
-    for far in (1, 2, 4, 8, 12, 14, 15):
+    for far in (1, 2, 3, 13, 14, 15):
         near = xl * 16 + (z + far) % 16
         pl.semaphore_signal(barrier, inc=1, device_id=(c, near), device_id_type=MESH)
 
@@ -168,25 +168,33 @@
         own_l[core] = jnp.where(first, l0, l1)
         sw_l[...] = jnp.where(first, l1, l0)
 
-    def z_copy(group, far, n, first_hand):
-        block = (z + 4 * group) % 16
-        src = lg_in if first_hand else ring.at[block]
+    def z_copy(back, far, n, rows, sem):
+        block = (z + 16 + back) % 16
+        ref = ring.at[block, rows, :]
+        src = lg_in if back == 0 else ref
         target = xl * 16 + (z + 16 + far) % 16
-        return remote(src, ring.at[block], rg_s.at[group, n], rg_r.at[block], (c, target))
-
-    z_first = [z_copy(0, far, n, True) for n, far in enumerate((4, -4, 8, 1, -1, 2))]
+        return remote(src, ref, rg_s.at[n], rg_r.at[block if sem is None else sem], (c, target))
+
+    z_all = pl.ds(0, SHARE)
+    z_half = (pl.ds(0, SHARE // 2), pl.ds(SHARE // 2, SHARE // 2))
+    z_first = [z_copy(0, far, n, z_all, None) for n, far in enumerate((3, -3, 1, -1))]
     z_later = [
-        [z_copy(group, far, n, False) for n, far in enumerate(fars)]
-        for group, fars in ((1, (1, -1, 2, -2)), (3, (-1, 1)), (2, (1, -1, -2)))
+        [z_copy(-3, far, 4 + n, z_all, None) for n, far in enumerate((3, 1, -1))],
+        [z_copy(3, far, 7 + n, z_all, None) for n, far in enumerate((-3, -1, 1))],
+        [z_copy(-6, far, 10 + n, z_all, None) for n, far in enumerate((1, -1))]
+        + [z_copy(-6, 2, 12, z_half[0], None)],
+        [z_copy(6, far, 13 + n, z_all, None) for n, far in enumerate((-1, 1))]
+        + [z_copy(6, -2, 15, z_half[1], 16)],
     ]
 
-    def z_arrived(block):
-        remote(ring.at[block], ring.at[block], rg_s.at[0, 0], rg_r.at[block], at_cp(sib)).wait_recv()
-
-    def z_pass():
-        for group, copies in zip((1, 3, 2), z_later):
-            z_arrived((z + 4 * group) % 16)
-            start(copies)
+    def z_arrived(block, rows, sem):
+        ref = ring.at[block, rows, :]
+        remote(ref, ref, rg_s.at[0], rg_r.at[sem], at_cp(sib)).wait_recv()
+
+    def z_pass(n):
+        block = (z + (13, 3, 10, 6)[n]) % 16
+        z_arrived(block, z_all, block)
+        start(z_later[n])
 
     swaps = [
         remote(sw_t, own_t.at[:, :, mine], sw_s.at[0], sw_r.at[0], at_cp(sib)),
@@ -275,9 +283,11 @@
         return carry
 
     def dispatch_all():
-        for block in range(1, 16):
-            if block % 4:
-                z_arrived((z + block) % 16)
+        for far in (1, 15, 2, 14, 4, 12, 5, 11, 7, 9):
+            z_arrived((z + far) % 16, z_all, (z + far) % 16)
+        opposite = (z + 8) % 16
+        z_arrived(opposite, z_half[0], opposite)
+        z_arrived(opposite, z_half[1], 16)
         lax.fori_loop(0, 8, dispatch, 0)
 
     def joined(rows, n):
@@ -362,7 +372,7 @@
         arrived(owner, half, col)
         to_sibling(owner, half, col, n + 4 * (1 - near))
 
-    pl.semaphore_wait(barrier, 30)
+    pl.semaphore_wait(barrier, 29)
     start(z_first)
     start(own_sends)
     stage()
@@ -393,13 +403,16 @@
         copy.wait_recv()
     start(att_sends)
     start([whole])
+    z_pass(0)
+    z_pass(1)
     relay_x(half_a, 0)
     relay_x(half_b, 1)
     relay_y(3, 1)
+    z_pass(2)
+    z_pass(3)
     relay_y(1, 1)
     att_relay(1)
     att_relay(3)
-    z_pass()
     att_relay(2)
     relay_y(3, 0)
     relay_y(1, 0)
@@ -473,12 +486,12 @@
         left[SHARE : 2 * SHARE, 128 * m : 128 * m + 128] = jnp.where(xl == 0, t1, t0)
 
     def product(n, carry):
-        tile = pl.ds(pl.multiple_of(n * 256, 256), 256)
-        right = hid[:, :, tile].reshape(16 * CAP, 256)
+        tile = pl.ds(pl.multiple_of(n * 512, 512), 512)
+        right = hid[:, :, tile].reshape(16 * CAP, 512)
         dg_ref[0, :, tile] = dot_nn(left[...], right).astype(BF16)
         return carry
 
-    lax.fori_loop(0, 8, product, 0)
+    lax.fori_loop(0, 4, product, 0)
 
     for copy in swaps + own_sends + fwd_sends + sib_sends + [whole] + att_sends + z_first + sum(z_later, []):
         copy.wait_send()
@@ -558,8 +571,8 @@
             dma((2, 8)),
             dma((2,)),
             dma((2,)),
-            dma((4, 6)),
             dma((16,)),
+            dma((17,)),
             dma((8, 2)),
             dma((16,)),
             dma((3, 4)),

time: 65.4 us -> 61.1 us (0.934)
  Pallas kernels: 64.6 us -> 60.3 us
    pallas_call x1, Pallas kernels: 61.6 us -> 57.3 us  [local(): pl.pallas_call(kernel, out_shape=shapes, in_specs=[hbm] * 10, out_specs=(...]
where the time goes in v3:
time: 61.1 us; the launch traced here: 61 us
  Pallas kernels  60.3 us (99%)
  between operations  0.64 us (1%)
    pallas_call x1, Pallas kernels, local(): pl.pallas_call(kernel, out_shape=shapes, in_specs=[hbm] * 10, out_specs=(...  57.3 us
    pallas_call x1, Pallas kernels, local(): pl.pallas_call(put_out, out_shape=shapes, in_specs=[vmem] * 4, out_specs=...  3.01 us

profile of v3, /device:TPU:7, one launch (start us, length us, event | category | flops | bytes accessed | tf_op | source)
XLA Modules:
  0.0 61.0 jit_solution(12888269826040434887)
XLA Ops:
  0.6 57.3 %shard_map.129 = (bf16[128,384]{1,0:T(8,128)(2,1)}, bf16[128,384]{1,0:T(8,128)(2,1)}, bf16[128,256]{1,0:T(8,128)(2,1)}, bf16[1,448,2048]{2,1,0:T(8,128)(2,1)}) custom-call(bf16[128,384]{1,0:T(8,128)(2,1)} %q_in.1, bf16[128,384]{1,0:T(8,128)(2,1)} %k_in.1, bf16[128,256]{1,0:T(8,128)(2,1)} %v_in.1, bf16[128,256]{1,0:T(8,128)(2,1)} %do_in.1, ...), custom_call_target="tpu_custom_call" | custom-call | tf_op jit(solution)/shard_map/pallas_call | solution.py:534
  58.0 3.0 %shard_map.130 = (bf16[128,384]{1,0:T(8,128)(2,1)}, bf16[128,384]{1,0:T(8,128)(2,1)}, bf16[128,256]{1,0:T(8,128)(2,1)}, bf16[1,448,2048]{2,1,0:T(8,128)(2,1)}) custom-call(bf16[128,384]{1,0:T(8,128)(2,1)} %get-tuple-element.12.refs_0_, bf16[128,384]{1,0:T(8,128)(2,1)} %get-tuple-element.13.refs_1_, bf16[128,256]{1,0:T(8,128)(2,1)} %get-tuple-element.14.refs_2_, ...), custom_call_target="tpu_custom_call" | custom-call | tf_op jit(solution)/shard_map/pallas_call | solution.py:588

commit v4 on v3

--- a/solution.py
+++ b/solution.py
@@ -38,7 +38,8 @@
     qg_ref,
     kg_ref,
     vg_ref,
-    dg_ref,
+    left,
+    hid,
     q_ref,
     k_ref,
     v_ref,
@@ -64,8 +65,6 @@
     ring,
     send,
     cols,
-    left,
-    hid,
     in_s,
     sw_s,
     sw_r,
@@ -485,14 +484,6 @@
         left[0:SHARE, 128 * m : 128 * m + 128] = jnp.where(xl == 0, t0, t1)
         left[SHARE : 2 * SHARE, 128 * m : 128 * m + 128] = jnp.where(xl == 0, t1, t0)
 
-    def product(n, carry):
-        tile = pl.ds(pl.multiple_of(n * 512, 512), 512)
-        right = hid[:, :, tile].reshape(16 * CAP, 512)
-        dg_ref[0, :, tile] = dot_nn(left[...], right).astype(BF16)
-        return carry
-
-    lax.fori_loop(0, 4, product, 0)
-
     for copy in swaps + own_sends + fwd_sends + sib_sends + [whole] + att_sends + z_first + sum(z_later, []):
         copy.wait_send()
 
@@ -512,13 +503,15 @@
     lax.fori_loop(0, 8, cols_sent, 0)
 
 
-def put_out(*refs):
-    ins, outs, sems = refs[0:4], refs[4:8], refs[8]
-    copies = [pltpu.make_async_copy(a, b, sems.at[n]) for n, (a, b) in enumerate(zip(ins, outs))]
-    for copy in copies:
-        copy.start()
-    for copy in copies:
-        copy.wait()
+def product(left, hid, q_in, k_in, v_in, q_out, k_out, v_out, out):
+    right = hid[...].reshape(16 * CAP, hid.shape[2])
+    out[0] = dot_nn(left[...], right).astype(BF16)
+
+    @pl.when(pl.program_id(0) == 0)
+    def _():
+        q_out[...] = q_in[...]
+        k_out[...] = k_in[...]
+        v_out[...] = v_in[...]
 
 
 def local(q, k, v, do, o, ln, lg, gp, ids, hidden):
@@ -529,13 +522,16 @@
         jax.ShapeDtypeStruct((128, 2 * QK), BF16),
         jax.ShapeDtypeStruct((128, 2 * QK), BF16),
         jax.ShapeDtypeStruct((128, 2 * DH), BF16),
-        jax.ShapeDtypeStruct((1, 2 * SHARE, 2048), BF16),
     )
-    results = pl.pallas_call(
+    q_part, k_part, v_part, left, rows = pl.pallas_call(
         kernel,
-        out_shape=shapes,
+        out_shape=shapes
+        + (
+            jax.ShapeDtypeStruct((2 * SHARE, 16 * CAP), BF16),
+            jax.ShapeDtypeStruct((16, CAP, 2048), BF16),
+        ),
         in_specs=[hbm] * 10,
-        out_specs=(vmem,) * 4,
+        out_specs=(vmem,) * 4 + (hbm,),
         scratch_shapes=[
             pltpu.VMEM((128, 2 * QK), BF16),
             pltpu.VMEM((128, 2 * QK), BF16),
@@ -562,8 +558,6 @@
             pltpu.VMEM((16, SHARE, 128), BF16),
             pltpu.VMEM((8, 2, SHARE, 128), BF16),
             pltpu.VMEM((16, SHARE, 128), BF16),
-            pltpu.VMEM((2 * SHARE, 16 * CAP), BF16),
-            pltpu.VMEM((16, CAP, 2048), BF16),
             dma((10,)),
             dma((2,)),
             dma((2,)),
@@ -585,13 +579,23 @@
             collective_id=0, has_side_effects=True, vmem_limit_bytes=60 * 2**20
         ),
     )(q, k, v, do, o, ln, lg.T, gp.T, ids.T, hidden)
+    def whole(*shape):
+        return pl.BlockSpec(shape, lambda n: (0,) * len(shape))
+
+    grads = [whole(128, 2 * QK), whole(128, 2 * QK), whole(128, 2 * DH)]
     q_grad, k_grad, v_grad, down = pl.pallas_call(
-        put_out,
-        out_shape=shapes,
-        in_specs=[vmem] * 4,
-        out_specs=(hbm,) * 4,
-        scratch_shapes=[dma((4,))],
-    )(*results)
+        product,
+        grid=(4,),
+        out_shape=shapes + (jax.ShapeDtypeStruct((1, 2 * SHARE, 2048), BF16),),
+        in_specs=[
+            whole(2 * SHARE, 16 * CAP),
+            pl.BlockSpec((16, CAP, 2048 // 4), lambda n: (0, 0, n)),
+        ]
+        + grads,
+        out_specs=tuple(grads)
+        + (pl.BlockSpec((1, 2 * SHARE, 2048 // 4), lambda n: (0, 0, n)),),
+        compiler_params=pltpu.CompilerParams(vmem_limit_bytes=60 * 2**20),
+    )(left, rows, q_part, k_part, v_part)
     return q_grad, k_grad, v_grad, jnp.swapaxes(down, 1, 2)
 
 

time: 61.1 us -> 60.2 us (0.985); the launches traced: 61 us -> 59.1 us
  Pallas kernels: 60.3 us -> 58.5 us
    pallas_call x2, Pallas kernels: 60.3 us -> 58.5 us  [the longest x1 52.6 us: local(): pl.pallas_call(kernel, out_shape=shapes + (jax.ShapeDtypeStruct((2 * SHAR...]
where the time goes in v4:
time: 60.2 us; the launch traced here: 59.1 us
  Pallas kernels  58.5 us (97%)
  between operations  0.64 us (1%)
    pallas_call x1, Pallas kernels, local(): pl.pallas_call(kernel, out_shape=shapes + (jax.ShapeDtypeStruct((2 * SHAR...  52.6 us
    pallas_call x1, Pallas kernels, local(): pl.pallas_call(product, grid=(4,), out_shape=shapes + (jax.ShapeDtypeStru...  5.91 us

profile of v4, /device:TPU:7, one launch (start us, length us, event | category | flops | bytes accessed | tf_op | source)
XLA Modules:
  0.0 59.1 jit_solution(13265011791689207724)
XLA Ops:
  0.6 52.6 %shard_map.129 = (bf16[128,384]{1,0:T(8,128)(2,1)}, bf16[128,384]{1,0:T(8,128)(2,1)}, bf16[128,256]{1,0:T(8,128)(2,1)}, bf16[448,1024]{1,0:T(8,128)(2,1)}, bf16[16,64,2048]{2,1,0:T(8,128)(2,1)}) custom-call(bf16[128,384]{1,0:T(8,128)(2,1)} %q_in.1, bf16[128,384]{1,0:T(8,128)(2,1)} %k_in.1, bf16[128,256]{1,0:T(8,128)(2,1)} %v_in.1, bf16[128,256]{1,0:T(8,128)(2,1)} %do_in.1, ...), custom_call_target="tpu_custom_call" | custom-call | tf_op jit(solution)/shard_map/pallas_call | solution.py:526
  53.2 5.9 %shard_map.130 = (bf16[128,384]{1,0:T(8,128)(2,1)}, bf16[128,384]{1,0:T(8,128)(2,1)}, bf16[128,256]{1,0:T(8,128)(2,1)}, bf16[1,448,2048]{2,1,0:T(8,128)(2,1)}) custom-call(bf16[448,1024]{1,0:T(8,128)(2,1)} %get-tuple-element.13.left, bf16[16,64,2048]{2,1,0:T(8,128)(2,1)} %get-tuple-element.14.hid, bf16[128,384]{1,0:T(8,128)(2,1)} %get-tuple-element.15.q_in, ...), custom_call_target="tpu_custom_call" | custom-call | tf_op jit(solution)/shard_map/pallas_call | solution.py:586
